TPU v7x, 512 devices: a whole 4x8x8 slice. The times are simulated.
512 devices in a mesh: ops: 64 (over x, z_lo, y), wf: 8 (over z_hi, core).
Axes of the slice: x: 4, y: 8, z: 8 (z_hi: 4, z_lo: 2; z = z_hi * 2 + z_lo), core: 2. Of those that a mesh axis runs over, the one named last changes fastest.
Arguments:
- psi_one: float32 [16, 512, 512], P('wf', 'ops'), may hold values from -6 to 6
- psi_two: float32 [16, 512, 512], P('wf', 'ops'), may hold values from -6 to 6
- left_ops: float32 [64, 16, 512, 512], P('ops', 'wf'), may hold values from -0.03125 to 0.03125
- right_ops: float32 [64, 16, 512, 512], P('ops', 'wf'), may hold values from -0.25 to 0.25
- shift_ops: float32 [16, 512, 512], P('wf'), may hold values from -0.25 to 0.25
- block_dims: int32 [16], replicated, may hold values from 64 to 512, as said below
- partner: int32 [16], replicated, may hold values from 0 to 15, each once
Outputs:
- sigma_one: float32 [16, 512, 512], P('wf', 'ops')
- sigma_two: float32 [16, 512, 512], P('wf', 'ops')
Inputs may be any that keep to these rules, and one draw needn't show every extreme that they name: `block_dims`: every block's live size; the largest block is 512 in every draw.
All inputs are finite; a program needn't handle non-finite values.
Results may differ from a plain program's by a relative error of at most 0.0001.
Values sent between devices are 32-bit elements; how exact they have to be, the bound alone decides.
No kernel may reach another device: no remote copies, remote signals or barrier semaphores. Data moves between devices by JAX's collectives and lax.ppermute only.
A program may use at most 64 MiB of HBM per device.

v0:
```python
import jax
import jax.numpy as jnp
from jax import lax
from jax.sharding import PartitionSpec as P


def per_device(psi_one, psi_two, left_ops, right_ops, shift_ops, block_dims, partner):
    highest = lax.Precision.HIGHEST
    local_blocks = psi_one.shape[0]
    rows = psi_one.shape[1]
    width = psi_one.shape[2]
    ops_index = lax.axis_index("ops")
    wf_index = lax.axis_index("wf")
    local_dims = lax.dynamic_slice_in_dim(block_dims, wf_index * local_blocks, local_blocks)
    local_pairs = lax.dynamic_slice_in_dim(partner, wf_index * local_blocks, local_blocks)
    columns = jnp.arange(width, dtype=jnp.int32)
    row_ids = ops_index * rows + jnp.arange(rows, dtype=jnp.int32)
    col_live = (columns[None, :] < local_dims[:, None]).astype(jnp.float32)
    row_live = (row_ids[None, :] < local_dims[:, None]).astype(jnp.float32)
    local_mask = row_live[:, :, None] * col_live[:, None, :]
    live_one = psi_one * local_mask
    live_two = psi_two * local_mask
    first = jnp.einsum(
        "tbik,bkj->tbij",
        left_ops,
        lax.all_gather(live_one, "ops", axis=1, tiled=True),
        precision=highest,
    )
    second = jnp.einsum(
        "tbik,bkj->tbij",
        left_ops,
        lax.all_gather(live_two, "ops", axis=1, tiled=True),
        precision=highest,
    )
    term_one = jnp.einsum("tbij,tblj->bil", first, right_ops, precision=highest)
    term_two = jnp.einsum("tbij,tblj->bil", second, right_ops, precision=highest)
    summed_one, summed_two = (
        lax.psum_scatter(term_one, "ops", scatter_dimension=1, tiled=True),
        lax.psum_scatter(term_two, "ops", scatter_dimension=1, tiled=True),
    )
    every_one, every_two = (
        lax.all_gather(live_one, "wf", axis=0, tiled=True),
        lax.all_gather(live_two, "wf", axis=0, tiled=True),
    )
    all_blocks = every_one.shape[0]
    select = (jnp.arange(all_blocks, dtype=jnp.int32)[None, :] == local_pairs[:, None]).astype(
        jnp.float32
    )
    paired_one = jnp.einsum("bn,nrp->brp", select, every_one, precision=highest)
    paired_two = jnp.einsum("bn,nrp->brp", select, every_two, precision=highest)
    shifted_one = jnp.einsum("brp,bqp->brq", paired_one, shift_ops, precision=highest)
    shifted_two = jnp.einsum("brp,bqp->brq", paired_two, shift_ops, precision=highest)
    sigma_one = (summed_one + shifted_one) * local_mask
    sigma_two = (summed_two + shifted_two) * local_mask
    return (sigma_one, sigma_two)


def solution(mesh):
    in_specs = (
        P("wf", "ops", None),
        P("wf", "ops", None),
        P("ops", "wf", None, None),
        P("ops", "wf", None, None),
        P("wf", None, None),
        P(),
        P(),
    )
    out_specs = (P("wf", "ops", None), P("wf", "ops", None))
    return jax.shard_map(
        per_device, mesh=mesh, in_specs=in_specs, out_specs=out_specs, check_vma=False
    )
```

profile of v0, /device:TPU:128, one launch (start us, length us, event | category | flops | bytes accessed | tf_op | source)
XLA Modules:
  0.0 1264.2 jit_solution(6103191122188067393)
XLA Ops:
  7.2 0.0 copy-start
  7.2 0.0 all-gather.5.cloned.1.call-start
  7.2 0.9 dynamic_slice.6
  8.1 0.1 compare_convert_fusion
  8.2 0.1 compare_convert_fusion.1
  8.3 1.5 multiply_multiply_fusion
  9.7 0.0 all-gather.5.cloned.1.call-update
  9.8 0.0 all-gather.3.cloned.1.call-start
  9.8 0.7 all-gather.3.cloned.1.call-update
  10.5 0.0 reduce-scatter.5.cloned.1.call-start
  10.6 306.1 %all-gather.5.cloned.1.call-done = f32[2,512,512]{2,1,0:T(8,128)} async-done(((f32[2,8,512]{2,1,0:T(8,128)}), f32[2,512,512]{2,1,0:T(8,128)}) %all-gather.5.cloned.1.call-update) | async-done | bytes 2097168 | tf_op jit(solution)/shard_map/all_gather | solution.py:32
  316.6 0.0 copy-done
  316.6 8.5 fusion.6
  325.1 8.4 fusion
  333.5 0.0 reduce-scatter.5.cloned.1.call-update
  333.5 0.0 reduce-scatter.3.cloned.1.call-start
  333.6 285.1 %all-gather.3.cloned.1.call-done = f32[2,512,512]{2,1,0:T(8,128)} async-done(((f32[2,8,512]{2,1,0:T(8,128)}), f32[2,512,512]{2,1,0:T(8,128)}) %all-gather.3.cloned.1.call-update) | async-done | bytes 2097168 | tf_op jit(solution)/shard_map/all_gather | solution.py:26
  618.6 8.5 fusion.8
  627.1 8.4 fusion.2
  635.5 0.0 reduce-scatter.3.cloned.1.call-update
  635.5 0.6 copy-done.5
  636.2 0.1 dynamic_slice.7
  636.2 0.0 copy-done.4
  636.3 14.8 %all_gather.15 = f32[16,8,512]{2,1,0:T(8,128)S(1)} all-gather(f32[2,8,512]{2,1,0:T(8,128)S(1)} %copy-done.4), channel_id=1, replica_groups=mesh['ops'=64,'wf'=8] {'wf'}, dimensions={0}, use_global_device_ids=true | all-gather | bytes 294912 | tf_op jit(solution)/shard_map/all_gather | solution.py:43
  651.0 0.0 copy-done.3
  651.0 14.7 %all_gather.13 = f32[16,8,512]{2,1,0:T(8,128)S(1)} all-gather(f32[2,8,512]{2,1,0:T(8,128)S(1)} %copy-done.3), channel_id=1, replica_groups=mesh['ops'=64,'wf'=8] {'wf'}, dimensions={0}, use_global_device_ids=true | all-gather | bytes 294912 | tf_op jit(solution)/shard_map/all_gather | solution.py:42
  665.7 0.4 fusion.12
  666.1 0.4 fusion.14
  666.4 271.3 %reduce-scatter.5.cloned.1.call-done = f32[2,8,512]{2,1,0:T(8,128)} async-done(((f32[2,512,512]{2,1,0:T(8,128)}), f32[2,8,512]{2,1,0:T(8,128)}) %reduce-scatter.5.cloned.1.call-update) | async-done | bytes 32784 | tf_op jit(solution)/shard_map/reduce_scatter | solution.py:39
  937.8 4.0 fusion.10
  941.8 311.9 %reduce-scatter.3.cloned.1.call-done = f32[2,8,512]{2,1,0:T(8,128)} async-done(((f32[2,512,512]{2,1,0:T(8,128)}), f32[2,8,512]{2,1,0:T(8,128)}) %reduce-scatter.3.cloned.1.call-update) | async-done | bytes 32784 | tf_op jit(solution)/shard_map/reduce_scatter | solution.py:38
  1253.7 4.0 fusion.11
  (8 shorter events, 0.0 us)
Async XLA Ops:
  7.2 309.5 %copy-start = (f32[1,2,512,512]{3,2,1,0:T(8,128)S(1)}, f32[1,2,512,512]{3,2,1,0:T(8,128)}, u32[]{:S(2)}) copy-start(f32[1,2,512,512]{3,2,1,0:T(8,128)} %param.9) | copy-start | bytes 6291460
  7.2 309.4 %all-gather.5.cloned.1.call-start = ((), (), s32[]{:S(2)}) async-start(), calls=%async_computation.4 | async-start | bytes 2129920 | tf_op jit(solution)/shard_map/all_gather | solution.py:32
  9.8 608.9 %all-gather.3.cloned.1.call-start = ((), (), s32[]{:S(2)}) async-start(), calls=%async_computation.2 | async-start | bytes 2129920 | tf_op jit(solution)/shard_map/all_gather | solution.py:26
  10.5 927.3 %reduce-scatter.5.cloned.1.call-start = ((), (), s32[]{:S(2)}) async-start(), calls=%async_computation.5 | async-start | bytes 2129920 | tf_op jit(solution)/shard_map/reduce_scatter | solution.py:39
  316.6 8.5 copy-start.1
  333.5 920.1 %reduce-scatter.3.cloned.1.call-start = ((), (), s32[]{:S(2)}) async-start(), calls=%async_computation.3 | async-start | bytes 2129920 | tf_op jit(solution)/shard_map/reduce_scatter | solution.py:38
  618.6 8.5 copy-start.2
  635.5 0.7 copy-start.5
  635.5 0.8 copy-start.4
  635.5 15.5 %copy-start.3 = (f32[2,8,512]{2,1,0:T(8,128)S(1)}, f32[2,8,512]{2,1,0:T(8,128)}, u32[]{:S(2)}) copy-start(f32[2,8,512]{2,1,0:T(8,128)} %get-tuple-element.3) | copy-start | bytes 98308
Sparse Core Ops, SparseCore 0:
  10.7 305.9 all-gather.4
  319.3 299.3 all-gather.2
  621.4 316.2 reduce-scatter.4
  940.6 312.9 reduce-scatter.2
where the time goes:
time: 1260 us
  waiting for transfers between devices  1180 us (94%)
  matrix products  42.4 us (3%)
  blocking collectives  29.4 us (2%)
  between operations  13.8 us (1%)
    reduce_scatter x1, waiting for transfers between devices, per_device(): lax.psum_scatter(term_one, 'ops', scatter_dimension=1, tiled=True)  312 us
    all_gather x1, waiting for transfers between devices, per_device(): lax.all_gather(live_two, 'ops', axis=1, tiled=True)  306 us
    all_gather x1, waiting for transfers between devices, per_device(): lax.all_gather(live_one, 'ops', axis=1, tiled=True)  285 us
    reduce_scatter x1, waiting for transfers between devices, per_device(): lax.psum_scatter(term_two, 'ops', scatter_dimension=1, tiled=True)  271 us
  transfers between devices with their start and end apart: 4, of which 4 were waited for; matrix products, arithmetic and copies ran while one was open for 3% of the time, Pallas kernels for 0%

commit v1 on v0

v1 whole, which is shorter than its diff:
```python
import jax
import jax.numpy as jnp
from jax import lax
from jax.sharding import Mesh, PartitionSpec as P

AXES = ("x", "zl", "yh", "yl", "zh", "c")
SIZES = (4, 2, 4, 2, 4, 2)
OPS = ("x", "zl", "yh", "yl")
WF = ("zh", "c")
FAR = ("zl", "yh")
NEAR = ("x", "yl")


def swap_pair(array):
    return lax.ppermute(array, "zl", [(0, 1), (1, 0)])


def per_device(psi_one, psi_two, left_ops, right_ops, shift_ops, block_dims, partner):
    high = lax.Precision.HIGH
    blocks, rows, width = psi_one.shape
    ops_index = lax.axis_index(OPS)
    wf_index = lax.axis_index(WF)
    mine = lax.axis_index("zl")

    local_dims = lax.dynamic_slice_in_dim(block_dims, wf_index * blocks, blocks)
    local_pairs = lax.dynamic_slice_in_dim(partner, wf_index * blocks, blocks)
    columns = jnp.arange(width, dtype=jnp.int32)
    row_ids = ops_index * rows + jnp.arange(rows, dtype=jnp.int32)
    col_live = columns[None, :] < local_dims[:, None]
    row_live = row_ids[None, :] < local_dims[:, None]
    mask = (row_live[:, :, None] & col_live[:, None, :]).astype(jnp.float32)
    live = jnp.stack([psi_one * mask, psi_two * mask], axis=1)

    other = 1 - mine
    left_in = swap_pair(lax.dynamic_index_in_dim(left_ops[0], other, 0, keepdims=False))
    right_in = swap_pair(lax.dynamic_index_in_dim(right_ops[0], other, 0, keepdims=False))
    left_own = lax.dynamic_index_in_dim(left_ops[0], mine, 0, keepdims=False)
    right_own = lax.dynamic_index_in_dim(right_ops[0], mine, 0, keepdims=False)

    far_out = jnp.broadcast_to(live[:, None], (2, 4, 2, rows, width)).reshape(8, 2, rows, width)
    far_in = lax.all_to_all(far_out, FAR, 0, 0, tiled=True)
    near_out = jnp.broadcast_to(far_in[None], (8,) + far_in.shape)
    near_in = lax.all_to_all(near_out, NEAR, 0, 0, tiled=True)

    full = near_in.reshape(4, 2, 2, 4, 2, rows, width)
    full = full.transpose(4, 0, 2, 3, 1, 5, 6).reshape(2, 64 * rows, width)

    total = 0.0
    for left, right in ((left_own, right_own), (left_in, right_in)):
        middle = jnp.einsum("ik,vkj->vij", left, full, precision=high)
        total = total + jnp.einsum("vij,lj->vil", middle, right, precision=high)

    near_back = total.reshape(2, 4, 2, 4, 2, rows, width).transpose(1, 4, 2, 3, 0, 5, 6)
    near_back = lax.all_to_all(near_back.reshape(8, 8, 2, rows, width), NEAR, 0, 0, tiled=True)
    near_sum = jnp.sum(near_back, axis=0)
    far_back = lax.all_to_all(near_sum, FAR, 0, 0, tiled=True)
    summed = jnp.sum(far_back.reshape(2, 4, 2, rows, width), axis=1)

    tied, unused = lax.optimization_barrier((live, near_in))
    every = lax.all_gather(tied, WF, axis=0, tiled=True)
    paired = jnp.take(every, local_pairs, axis=0, mode="clip")
    shifted = jnp.einsum("bvrp,bqp->bvrq", paired, shift_ops, precision=high)

    sigma = (summed + shifted) * mask[:, None]
    return sigma[:, 0], sigma[:, 1]


def solution(mesh):
    fine = Mesh(mesh.devices.reshape(SIZES), AXES)
    in_specs = (
        P(WF, OPS, None),
        P(WF, OPS, None),
        P(OPS, WF, None, None),
        P(OPS, WF, None, None),
        P(WF, None, None),
        P(),
        P(),
    )
    out_specs = (P(WF, OPS, None), P(WF, OPS, None))
    return jax.shard_map(
        per_device, mesh=fine, in_specs=in_specs, out_specs=out_specs, check_vma=False
    )
```

time: 1260 us -> 148 us (0.12)
  the two profiles are of different devices: /device:TPU:128 before, /device:TPU:41 now
where the time goes in v1:
time: 148 us; the launch traced here: 147 us
  waiting for transfers between devices  52.2 us (35%)
  blocking collectives  37.7 us (25%)
  starting transfers between devices  25.4 us (17%)
  matrix products  18 us (12%)
  local copies, waits for them, and re-layouts  9.17 us (6%)
  other arithmetic  3.63 us (2%)
    all_gather x1, blocking collectives, per_device(): every = lax.all_gather(tied, WF, axis=0, tiled=True)  24.3 us
    all_to_all x1, waiting for transfers between devices, per_device(): lax.all_to_all(near_back.reshape(8, 8, 2, rows, width), NEAR, 0, 0, tiled...  24 us
    all_to_all x1, waiting for transfers between devices, per_device(): near_in = lax.all_to_all(near_out, NEAR, 0, 0, tiled=True)  18.2 us
    all_to_all x1, blocking collectives, per_device(): far_in = lax.all_to_all(far_out, FAR, 0, 0, tiled=True)  13.4 us
    ppermute x2, waiting for transfers between devices, swap_pair(): return lax.ppermute(array, 'zl', [(0, 1), (1, 0)])  10 us
    dot_general x2, matrix products, per_device(): middle = jnp.einsum('ik,vkj->vij', left, full, precision=high)  8.27 us
    all_to_all x1, starting transfers between devices, per_device(): near_in = lax.all_to_all(near_out, NEAR, 0, 0, tiled=True)  8.19 us
    dot_general x2, matrix products, per_device(): total = total + jnp.einsum('vij,lj->vil', middle, right, precision=high)  7.22 us
  transfers between devices with their start and end apart: 5, of which 3 were waited for; matrix products, arithmetic and copies ran while one was open for 11% of the time, Pallas kernels for 0%

profile of v1, /device:TPU:41, one launch (start us, length us, event | category | flops | bytes accessed | tf_op | source)
XLA Modules:
  0.0 147.0 jit_solution(4203711944305906226)
XLA Ops:
  0.6 0.0 copy-start
  0.7 0.9 dynamic_slice.19
  1.5 0.1 iota_compare_fusion
  1.6 0.1 broadcast_compare_fusion
  1.7 0.8 fusion.23
  2.6 13.4 %all_to_all.20 = f32[8,2,8,512]{3,2,1,0:T(8,128)S(1)} all-to-all(f32[8,2,8,512]{3,2,1,0:T(8,128)S(1)} %bitcast.63), channel_id=1, replica_groups=mesh['x'=4,'zl'=2,'yh'=4,'yl'=2,'zh'=4,'c'=2] {'zl','yh'}, dimensions={0} | all-to-all | bytes 524288 | tf_op jit(solution)/shard_map/all_to_all | solution.py:41
  16.0 1.6 %broadcast_in_dim.8 = f32[8,8,2,8,512]{4,3,2,1,0:T(8,128)} broadcast(f32[8,2,8,512]{3,2,1,0:T(8,128)S(1)} %all_to_all.20), dimensions={1,2,3,4} | broadcast | bytes 2359296 | tf_op jit(solution)/shard_map/broadcast_in_dim | solution.py:42
  17.6 8.2 %all-to-all-start.1 = ((f32[8,8,2,8,512]{4,3,2,1,0:T(8,128)}), f32[8,8,2,8,512]{4,3,2,1,0:T(8,128)}, u32[]{:S(2)}, u32[]{:S(2)}) async-start(f32[8,8,2,8,512]{4,3,2,1,0:T(8,128)} %broadcast_in_dim.8), calls=%async_computation.1 | async-start | bytes 4194304 | tf_op jit(solution)/shard_map/all_to_all | solution.py:43
  25.7 1.0 dynamic-slice_bitcast_fusion.1
  26.8 2.1 %collective-permute-start = (f32[512,512]{1,0:T(8,128)}, f32[512,512]{1,0:T(8,128)}, u32[]{:S(2)}, u32[]{:S(2)}) collective-permute-start(f32[512,512]{1,0:T(8,128)} %dynamic-slice_bitcast_fusion.1), channel_id=1, source_target_pairs={{0,64},{64,0},{1,65},{65,1},{2,66},{66,2},{3,67},{67,3},{4,68},{68... | collective-permute-start | bytes 3145736 | tf_op jit(solution)/shard_map/ppermute | solution.py:15
  28.9 1.1 dynamic-slice_bitcast_fusion
  29.9 3.2 %collective-permute-start.1 = (f32[512,512]{1,0:T(8,128)}, f32[512,512]{1,0:T(8,128)S(1)}, u32[]{:S(2)}, u32[]{:S(2)}) collective-permute-start(f32[512,512]{1,0:T(8,128)} %dynamic-slice_bitcast_fusion), channel_id=1, source_target_pairs={{0,64},{64,0},{1,65},{65,1},{2,66},{66,2},{3,67},{67,3},{4,68},{68... | collective-permute-start | bytes 3145736 | tf_op jit(solution)/shard_map/ppermute | solution.py:15
  33.1 18.2 %all-to-all-done.1 = f32[8,8,2,8,512]{4,3,2,1,0:T(8,128)} async-done(((f32[8,8,2,8,512]{4,3,2,1,0:T(8,128)}), f32[8,8,2,8,512]{4,3,2,1,0:T(8,128)}, u32[]{:S(2)}, u32[]{:S(2)}) %all-to-all-start.1) | async-done | bytes 2097184 | tf_op jit(solution)/shard_map/all_to_all | solution.py:43
  51.3 1.8 %copy.20 = f32[2,4,2,4,2,8,512]{6,5,4,3,2,1,0:T(8,128)S(1)} copy(f32[2,4,2,4,2,8,512]{6,5,0,3,2,4,1:T(8,128)} %bitcast.4) | data formatting | bytes 4194304 | tf_op jit(solution)/shard_map/transpose | solution.py:46
  53.1 0.0 copy-start.2
  53.2 3.5 %fusion.16 = f32[2,512,512]{2,1,0:T(8,128)S(1)} fusion(f32[2,512,512]{2,1,0:T(8,128)S(1)} %bitcast.59, f32[1,2,512,512]{3,2,1,0:T(8,128)S(1)} %copy-done, s32[]{:T(128)S(6)} %select_n.14), kind=kOutput, calls=%fused_computation.11 | convolution fusion | flops 1610612736 | bytes 5242884 | tf_op jit(solution)/shard_map/ik,vkj->vij/dot_general | solution.py:50
  56.7 3.5 %fusion.4 = f32[2,512,512]{2,1,0:T(8,128)S(1)} fusion(f32[2,512,512]{2,1,0:T(8,128)S(1)} %fusion.16, f32[1,2,512,512]{3,2,1,0:T(8,128)S(1)} %copy-done.2, s32[]{:T(128)S(6)} %select_n.14), kind=kOutput, calls=%fused_computation.5 | convolution fusion | flops 1610612736 | bytes 5242884 | tf_op jit(solution)/shard_map/vij,lj->vil/dot_general | solution.py:51
  60.2 0.0 collective-permute-done
  60.2 4.7 %fusion.19 = f32[2,512,512]{2,1,0:T(8,128)S(1)} fusion(f32[2,512,512]{2,1,0:T(8,128)S(1)} %bitcast.60, f32[512,512]{1,0:T(8,128)} %collective-permute-done), kind=kOutput, calls=%fused_computation.14 | convolution fusion | flops 1610612736 | bytes 5242880 | tf_op jit(solution)/shard_map/ik,vkj->vij/dot_general | solution.py:50
  65.0 10.0 %collective-permute-done.1 = f32[512,512]{1,0:T(8,128)S(1)} collective-permute-done((f32[512,512]{1,0:T(8,128)}, f32[512,512]{1,0:T(8,128)S(1)}, u32[]{:S(2)}, u32[]{:S(2)}) %collective-permute-start.1) | collective-permute-done | bytes 1048608 | tf_op jit(solution)/shard_map/ppermute | solution.py:15
  75.0 3.7 %fusion.6 = f32[2,512,512]{2,1,0:T(8,128)S(1)} fusion(f32[2,512,512]{2,1,0:T(8,128)S(1)} %fusion.4, f32[2,512,512]{2,1,0:T(8,128)S(1)} %fusion.19, f32[512,512]{1,0:T(8,128)S(1)} %collective-permute-done.1), kind=kOutput, calls=%fused_computation.7 | convolution fusion | flops 1611137024 | bytes 7340032 | tf_op jit(solution)/shard_map/vij,lj->vil/dot_general | solution.py:51
  78.7 1.5 %copy.25 = f32[2,4,2,4,2,8,512]{6,5,0,3,2,4,1:T(8,128)} copy(f32[2,4,2,4,2,8,512]{6,5,4,3,2,1,0:T(8,128)S(1)} %bitcast.61) | data formatting | bytes 4194304 | tf_op jit(solution)/shard_map/reshape | solution.py:53
  80.3 5.3 %all-to-all-start.2 = ((f32[8,8,2,8,512]{4,3,2,1,0:T(8,128)}), f32[8,8,2,8,512]{4,3,2,1,0:T(8,128)}, u32[]{:S(2)}, u32[]{:S(2)}) async-start(f32[8,8,2,8,512]{4,3,2,1,0:T(8,128)} %bitcast.62), calls=%async_computation.2 | async-start | bytes 4194304 | tf_op jit(solution)/shard_map/all_to_all | solution.py:54
  85.6 0.1 dynamic_slice.24
  85.7 24.0 %all-to-all-done.2 = f32[8,8,2,8,512]{4,3,2,1,0:T(8,128)} async-done(((f32[8,8,2,8,512]{4,3,2,1,0:T(8,128)}), f32[8,8,2,8,512]{4,3,2,1,0:T(8,128)}, u32[]{:S(2)}, u32[]{:S(2)}) %all-to-all-start.2) | async-done | bytes 2097184 | tf_op jit(solution)/shard_map/all_to_all | solution.py:54
  109.6 2.5 %reduce_sum.18 = f32[8,2,8,512]{3,2,1,0:T(8,128)} reduce(f32[8,8,2,8,512]{4,3,2,1,0:T(8,128)} %all-to-all-done.2, f32[]{:T(128)} %constant.50.clone.1), dimensions={0}, to_apply=%region_0.1 | reduce | flops 458752 | bytes 2359300 | tf_op jit(solution)/shard_map/reduce_sum | solution.py:55
  112.2 6.6 %all-to-all-start.3 = ((f32[8,2,8,512]{3,2,1,0:T(8,128)}), f32[8,2,8,512]{3,2,1,0:T(8,128)S(1)}, u32[]{:S(2)}, u32[]{:S(2)}) async-start(f32[8,2,8,512]{3,2,1,0:T(8,128)} %reduce_sum.18), calls=%async_computation.3 | async-start | bytes 524288 | tf_op jit(solution)/shard_map/all_to_all | solution.py:56
  118.8 0.1 and_convert_fusion
  118.9 24.3 %all_gather.3 = f32[16,2,8,512]{3,2,0,1:T(8,128)S(1)} all-gather(f32[2,2,8,512]{3,2,0,1:T(8,128)S(1)} %pad_maximum_fusion), channel_id=1, replica_groups=mesh['x'=4,'zl'=2,'yh'=4,'yl'=2,'zh'=4,'c'=2] {'zh','c'}, dimensions={0}, use_global_device_ids=true | all-gather | bytes 589824 | tf_op jit(solution)/shard_map/all_gather | solution.py:60
  143.2 0.5 gather_fusion
  143.8 2.5 %fusion.12 = f32[2,2,8,512]{3,2,1,0:T(8,128)S(1)} fusion(f32[2,2,8,512]{3,2,1,0:T(8,128)S(1)} %bitcast_reduce_fusion, f32[2,2,8,512]{3,2,1,0:T(8,128)S(1)} %gather_fusion, f32[2,512,512]{2,1,0:T(8,128)} %param.11, f32[2,8,512]{2,1,0:T(8,128)S(1)} %and_convert_fusion), kind=kOutput, calls=%fused_computation.9 | convolution fusion | flops 50364416 | bytes 2326528 | tf_op jit(solution)/shard_map/bvrp,bqp->bvrq/dot_general | solution.py:62
  146.4 0.6 slice_bitcast_fusion
  (13 shorter events, 0.1 us)
Async XLA Ops:
  0.6 25.1 %copy-start = (f32[1,2,512,512]{3,2,1,0:T(8,128)S(1)}, f32[1,2,512,512]{3,2,1,0:T(8,128)}, u32[]{:S(2)}) copy-start(f32[1,2,512,512]{3,2,1,0:T(8,128)} %param.9) | copy-start | bytes 6291460
  17.6 33.8 %all-to-all-start.1 = ((f32[8,8,2,8,512]{4,3,2,1,0:T(8,128)}), f32[8,8,2,8,512]{4,3,2,1,0:T(8,128)}, u32[]{:S(2)}, u32[]{:S(2)}) async-start(f32[8,8,2,8,512]{4,3,2,1,0:T(8,128)} %broadcast_in_dim.8), calls=%async_computation.1 | async-start | bytes 4194304 | tf_op jit(solution)/shard_map/all_to_all | solution.py:43
  25.7 3.1 %copy-start.1 = (f32[1,2,512,512]{3,2,1,0:T(8,128)S(1)}, f32[1,2,512,512]{3,2,1,0:T(8,128)}, u32[]{:S(2)}) copy-start(f32[1,2,512,512]{3,2,1,0:T(8,128)} %param.10) | copy-start | bytes 6291460
  26.8 33.5 %collective-permute-start = (f32[512,512]{1,0:T(8,128)}, f32[512,512]{1,0:T(8,128)}, u32[]{:S(2)}, u32[]{:S(2)}) collective-permute-start(f32[512,512]{1,0:T(8,128)} %dynamic-slice_bitcast_fusion.1), channel_id=1, source_target_pairs={{0,64},{64,0},{1,65},{65,1},{2,66},{66,2},{3,67},{67,3},{4,68},{68... | collective-permute-start | bytes 3145736 | tf_op jit(solution)/shard_map/ppermute | solution.py:15
  29.9 45.1 %collective-permute-start.1 = (f32[512,512]{1,0:T(8,128)}, f32[512,512]{1,0:T(8,128)S(1)}, u32[]{:S(2)}, u32[]{:S(2)}) collective-permute-start(f32[512,512]{1,0:T(8,128)} %dynamic-slice_bitcast_fusion), channel_id=1, source_target_pairs={{0,64},{64,0},{1,65},{65,1},{2,66},{66,2},{3,67},{67,3},{4,68},{68... | collective-permute-start | bytes 3145736 | tf_op jit(solution)/shard_map/ppermute | solution.py:15
  53.1 3.6 %copy-start.2 = (f32[1,2,512,512]{3,2,1,0:T(8,128)S(1)}, f32[1,2,512,512]{3,2,1,0:T(8,128)}, u32[]{:S(2)}) copy-start(f32[1,2,512,512]{3,2,1,0:T(8,128)} %param.10) | copy-start | bytes 6291460
  80.3 5.3 %copy-start.3 = (s32[16]{0:T(128)S(1)}, s32[16]{0:T(128)}, u32[]{:S(2)}) copy-start(s32[16]{0:T(128)} %param.13) | copy-start | bytes 196
  80.3 29.4 %all-to-all-start.2 = ((f32[8,8,2,8,512]{4,3,2,1,0:T(8,128)}), f32[8,8,2,8,512]{4,3,2,1,0:T(8,128)}, u32[]{:S(2)}, u32[]{:S(2)}) async-start(f32[8,8,2,8,512]{4,3,2,1,0:T(8,128)} %bitcast.62), calls=%async_computation.2 | async-start | bytes 4194304 | tf_op jit(solution)/shard_map/all_to_all | solution.py:54
  112.2 31.6 %all-to-all-start.3 = ((f32[8,2,8,512]{3,2,1,0:T(8,128)}), f32[8,2,8,512]{3,2,1,0:T(8,128)S(1)}, u32[]{:S(2)}, u32[]{:S(2)}) async-start(f32[8,2,8,512]{3,2,1,0:T(8,128)} %reduce_sum.18), calls=%async_computation.3 | async-start | bytes 524288 | tf_op jit(solution)/shard_map/all_to_all | solution.py:56

commit v2 on v1

v2 whole, which is shorter than its diff:
```python
import jax
import jax.numpy as jnp
from jax import lax
from jax.experimental import pallas as pl
from jax.experimental.pallas import tpu as pltpu
from jax.sharding import Mesh, PartitionSpec as P

AXES = ("x", "zl", "yh", "yl", "zh", "c")
SIZES = (4, 2, 4, 2, 4, 2)
OPS = ("x", "zl", "yh", "yl")
WF = ("zh", "c")
FAR = ("zl", "yh")
NEAR = ("x", "yl")
F32 = jnp.float32
BF16 = jnp.bfloat16
VMEM = pl.BlockSpec(memory_space=pltpu.VMEM)
SMEM = pl.BlockSpec(memory_space=pltpu.SMEM)
PARAMS = pltpu.CompilerParams(vmem_limit_bytes=48 * 1024 * 1024)


def shape(*dims):
    return jax.ShapeDtypeStruct(dims, F32)


def halves(value):
    high = value.astype(BF16)
    return high, (value - high.astype(F32)).astype(BF16)


def times(a, b):
    return jnp.dot(a, b, preferred_element_type=F32)


def times_t(a, b):
    return lax.dot_general(a, b, (((1,), (1,)), ((), ())), preferred_element_type=F32)


def live_mask(place_ref, dims_ref, block, rows, width):
    size = dims_ref[place_ref[1] * 2 + block]
    row = place_ref[0] * rows + lax.broadcasted_iota(jnp.int32, (rows, width), 0)
    column = lax.broadcasted_iota(jnp.int32, (rows, width), 1)
    return (row < size) & (column < size)


def swap(value):
    return lax.ppermute(value, "zl", [(0, 1), (1, 0)])


def after(value, earlier):
    return lax.optimization_barrier((value, earlier))[0]


def spread_kernel(place_ref, dims_ref, one_ref, two_ref, keep_ref, send_ref, live_ref):
    blocks, rows, width = one_ref.shape
    mine = place_ref[0] // 8 % 2
    for ref, block in ((keep_ref, mine), (send_ref, 1 - mine)):
        mask = live_mask(place_ref, dims_ref, block, rows, width)
        for vector, psi_ref in enumerate((one_ref, two_ref)):
            live = jnp.where(mask, psi_ref[block], 0.0)
            ref[vector] = live
            live_ref[block, vector] = live


def product_kernel(
    mine_ref, g_ref, l_ref, r_ref, l_in_ref, r_in_ref, out_ref, ph, pw, mh, ml, rh, rl
):
    width = g_ref.shape[-1]
    half = width // 2
    for x in range(4):
        for z in range(2):
            part = g_ref[x, :, :, (z + mine_ref[0]) % 2, 0].transpose(1, 0, 2, 3).reshape(64, width)
            rows = pl.ds(x * 128 + z * 64, 64)
            ph[rows], pw[rows] = halves(part)
    for t, (left, right) in enumerate(
        ((l_ref.at[0, 0], r_ref.at[0, 0]), (l_in_ref, r_in_ref))
    ):
        for i in range(2):
            rows = pl.ds(i * half, half)
            high, low = halves(left[rows])
            m = times(high, ph[...]) + times(low, ph[...]) + times(high, pw[...])
            mh[t, rows], ml[t, rows] = halves(m)
            rh[t, rows], rl[t, rows] = halves(right[rows])
    for i in range(2):
        rows = pl.ds(i * half, half)
        s = times_t(mh[0, rows], rh[0]) + times_t(ml[0, rows], rh[0]) + times_t(mh[0, rows], rl[0])
        s += times_t(mh[1, rows], rh[1]) + times_t(ml[1, rows], rh[1]) + times_t(mh[1, rows], rl[1])
        s = s.reshape(2, 2, 4, 2, 8, width).transpose(0, 3, 1, 2, 4, 5)
        out_ref[pl.ds(i * 2, 2)] = s


def sum_kernel(one_ref, two_ref, out_ref):
    for vector, ref in enumerate((one_ref, two_ref)):
        total = ref[0]
        for source in range(1, ref.shape[0]):
            total = total + ref[source]
        out_ref[:, vector] = total


def shift_kernel(place_ref, pair_ref, *refs):
    every, (shift_ref, out_ref) = refs[:4], refs[4:]
    blocks, width = shift_ref.shape[0], shift_ref.shape[-1]
    for block in range(blocks):
        pair = pair_ref[place_ref[1] * 2 + block]
        owner = pair // 2
        step = (owner // 2 - place_ref[1] // 2 + 4) % 4
        core = (owner + place_ref[1]) % 2
        paired = every[0][core, pair % 2]
        for other in range(1, 4):
            paired = jnp.where(step == other, every[other][core, pair % 2], paired)
        high, low = halves(paired.reshape(16, width))
        s_high, s_low = halves(shift_ref[block])
        out = times_t(high, s_high) + times_t(low, s_high) + times_t(high, s_low)
        out_ref[block] = out.reshape(2, 8, width)


def final_kernel(place_ref, dims_ref, back_ref, shifted_ref, one_ref, two_ref):
    blocks, rows, width = one_ref.shape
    for block in range(blocks):
        mask = live_mask(place_ref, dims_ref, block, rows, width)
        for vector, ref in enumerate((one_ref, two_ref)):
            total = shifted_ref[block, vector]
            for source in range(4):
                total = total + back_ref[block * 4 + source, vector]
            ref[block] = jnp.where(mask, total, 0.0)


def per_device(psi_one, psi_two, left_ops, right_ops, shift_ops, block_dims, partner):
    blocks, rows, width = psi_one.shape
    place = jnp.stack([lax.axis_index(OPS), lax.axis_index(WF)]).astype(jnp.int32)

    keep, send, live = pl.pallas_call(
        spread_kernel,
        out_shape=(shape(2, rows, width), shape(2, rows, width), shape(2, 2, rows, width)),
        in_specs=[SMEM, SMEM, VMEM, VMEM],
        out_specs=(VMEM, VMEM, VMEM),
        compiler_params=PARAMS,
        name="spread",
    )(place, block_dims, psi_one, psi_two)

    mine = lax.axis_index("zl").astype(jnp.int32)
    got = swap(send)
    left_out = lax.dynamic_index_in_dim(left_ops[0], 1 - mine, 0, keepdims=False)
    right_out = lax.dynamic_index_in_dim(right_ops[0], 1 - mine, 0, keepdims=False)
    got, left_out, right_out = lax.optimization_barrier((got, left_out, right_out))
    left_in = swap(left_out)
    right_in = swap(right_out)
    mine = mine[None]

    far_out = jnp.broadcast_to(jnp.stack([keep, got])[None], (4, 2, 2, rows, width))
    far_in = lax.all_to_all(far_out, "yh", 0, 0, tiled=True)

    other_core = lax.ppermute(live, "c", [(0, 1), (1, 0)])
    far_in, other_core = lax.optimization_barrier((far_in, other_core))

    near_out = jnp.broadcast_to(far_in[None], (8, 4, 2, 2, rows, width))
    near_in = lax.cond(
        lax.optimization_barrier(jnp.bool_(True)),
        lambda value: lax.all_to_all(value, NEAR, 0, 0, tiled=True),
        lambda value: value,
        near_out,
    )
    near_in, left_in, right_in = lax.optimization_barrier((near_in, left_in, right_in))

    near_backs = []
    for vector in range(2):
        sums = pl.pallas_call(
            product_kernel,
            out_shape=shape(4, 2, 2, 4, rows, width),
            grid_spec=pltpu.PrefetchScalarGridSpec(
                num_scalar_prefetch=1,
                grid=(1,),
                in_specs=[
                    pl.BlockSpec(
                        (4, 2, 4, 2, 1, rows, width),
                        lambda i, mine, vector=vector: (0, 0, 0, 0, vector, 0, 0),
                    ),
                    pl.BlockSpec((1, 1, width, width), lambda i, mine: (0, mine[0], 0, 0)),
                    pl.BlockSpec((1, 1, width, width), lambda i, mine: (0, mine[0], 0, 0)),
                    pl.BlockSpec((width, width), lambda i, mine: (0, 0)),
                    pl.BlockSpec((width, width), lambda i, mine: (0, 0)),
                ],
                out_specs=pl.BlockSpec(
                    (4, 2, 2, 4, rows, width), lambda i, mine: (0, 0, 0, 0, 0, 0)
                ),
                scratch_shapes=[
                    pltpu.VMEM((width, width), BF16),
                    pltpu.VMEM((width, width), BF16),
                    pltpu.VMEM((2, width, width), BF16),
                    pltpu.VMEM((2, width, width), BF16),
                    pltpu.VMEM((2, width, width), BF16),
                    pltpu.VMEM((2, width, width), BF16),
                ],
            ),
            compiler_params=PARAMS,
            cost_estimate=pl.CostEstimate(
                flops=12 * 2 * 512**3, bytes_accessed=8 * 2**20, transcendentals=0
            ),
            name="products",
        )(
            mine,
            near_in.reshape(4, 2, 4, 2, 2, rows, width),
            left_ops,
            right_ops,
            left_in,
            right_in,
        )

        near_backs.append(
            lax.all_to_all(sums.reshape(8, 8, rows, width), NEAR, 0, 0, tiled=True)
        )

    chip = after(jnp.stack([live, other_core]), near_in)
    every = [chip] + [
        lax.ppermute(chip, "zh", [((i + step) % 4, i) for i in range(4)]) for step in (1, 2, 3)
    ]

    near_sum = pl.pallas_call(
        sum_kernel,
        out_shape=shape(8, 2, rows, width),
        in_specs=[VMEM, VMEM],
        out_specs=VMEM,
        compiler_params=PARAMS,
        name="near_sum",
    )(*near_backs)
    near_sum, every[1], every[2] = lax.optimization_barrier((near_sum, every[1], every[2]))
    far_back = lax.all_to_all(near_sum, FAR, 0, 0, tiled=True)

    shifted = pl.pallas_call(
        shift_kernel,
        out_shape=shape(blocks, 2, rows, width),
        in_specs=[SMEM, SMEM, VMEM, VMEM, VMEM, VMEM, VMEM],
        out_specs=VMEM,
        compiler_params=PARAMS,
        cost_estimate=pl.CostEstimate(
            flops=3 * 2 * 32 * 512**2, bytes_accessed=3 * 2**20, transcendentals=0
        ),
        name="shift",
    )(place, partner, *every, shift_ops)

    return pl.pallas_call(
        final_kernel,
        out_shape=(shape(blocks, rows, width), shape(blocks, rows, width)),
        in_specs=[SMEM, SMEM, VMEM, VMEM],
        out_specs=(VMEM, VMEM),
        compiler_params=PARAMS,
        name="finish",
    )(place, block_dims, far_back, shifted)


def solution(mesh):
    fine = Mesh(mesh.devices.reshape(SIZES), AXES)
    in_specs = (
        P(WF, OPS, None),
        P(WF, OPS, None),
        P(OPS, WF, None, None),
        P(OPS, WF, None, None),
        P(WF, None, None),
        P(),
        P(),
    )
    out_specs = (P(WF, OPS, None), P(WF, OPS, None))
    return jax.shard_map(
        per_device, mesh=fine, in_specs=in_specs, out_specs=out_specs, check_vma=False
    )
```

time: 148 us -> 133 us (0.90)
  the two profiles are of different devices: /device:TPU:41 before, /device:TPU:2 now
where the time goes in v2:
time: 133 us; the launch traced here: 132 us
  starting transfers between devices  52.3 us (39%)
  blocking collectives  27.3 us (21%)
  waiting for transfers between devices  23.6 us (18%)
  Pallas kernels  17.3 us (13%)
  local copies, waits for them, and re-layouts  10.6 us (8%)
    all_to_all x1, blocking collectives, per_device(): lax.all_to_all(value, NEAR, 0, 0, tiled=True)  27.3 us
    ppermute x3, starting transfers between devices, per_device(): lax.ppermute(chip, 'zh', [((i + step) % 4, i) for i in range(4)])  17.2 us
    pallas_call x2, Pallas kernels, per_device(): pl.pallas_call(product_kernel, out_shape=shape(4, 2, 2, 4, rows, width),...  13.2 us
    ppermute x3, waiting for transfers between devices, per_device(): lax.ppermute(chip, 'zh', [((i + step) % 4, i) for i in range(4)])  12.5 us
    all_to_all x2, starting transfers between devices, per_device(): lax.all_to_all(sums.reshape(8, 8, rows, width), NEAR, 0, 0, tiled=True)  11.1 us
    ppermute x3, starting transfers between devices, swap(): return lax.ppermute(value, 'zl', [(0, 1), (1, 0)])  10.1 us
    all_to_all x1, starting transfers between devices, per_device(): far_in = lax.all_to_all(far_out, 'yh', 0, 0, tiled=True)  7.09 us
    all_to_all x1, waiting for transfers between devices, per_device(): far_in = lax.all_to_all(far_out, 'yh', 0, 0, tiled=True)  6.58 us
  transfers between devices with their start and end apart: 11, of which 6 were waited for; matrix products, arithmetic and copies ran while one was open for 4% of the time, Pallas kernels for 7%

profile of v2, /device:TPU:2, one launch (start us, length us, event | category | flops | bytes accessed | tf_op | source)
XLA Modules:
  0.0 131.8 jit_solution(7619549219639173227)
XLA Ops:
  0.7 0.8 copy-done.2
  1.5 0.8 copy-done.3
  2.2 0.7 copy-done.4
  3.5 4.3 %collective-permute-start = (f32[2,8,512]{2,1,0:T(8,128)S(1)}, f32[2,8,512]{2,1,0:T(8,128)S(1)}, u32[]{:S(2)}, u32[]{:S(2)}) collective-permute-start(f32[2,8,512]{2,1,0:T(8,128)S(1)} %get-tuple-element.23), channel_id=1, source_target_pairs={{0,64},{64,0},{1,65},{65,1},{2,66},{66,2},{3,67},{67,3},{4,68},{68... | collective-permute-start | bytes 98312 | tf_op jit(solution)/shard_map/ppermute | solution.py:46
  7.8 2.7 %dynamic-slice_bitcast_fusion = (f32[512,512]{1,0:T(8,128)S(1)}, f32[512,512]{1,0:T(8,128)}) fusion(f32[1,2,512,512]{3,2,1,0:T(8,128)} %r_ref.3, s32[]{:T(128)S(6)} %select_n.5, f32[1,2,512,512]{3,2,1,0:T(8,128)} %l_ref.3), kind=kLoop, calls=%fused_computation | loop fusion | bytes 4194308 | tf_op jit(solution)/shard_map/jit(dynamic_index_in_dim)/squeeze | solution.py:143
  10.5 3.1 %collective-permute-start.2 = (f32[512,512]{1,0:T(8,128)}, f32[512,512]{1,0:T(8,128)}, u32[]{:S(2)}, u32[]{:S(2)}) collective-permute-start(f32[512,512]{1,0:T(8,128)} %get-tuple-element.27), channel_id=1, source_target_pairs={{0,64},{64,0},{1,65},{65,1},{2,66},{66,2},{3,67},{67,3},{4,68},{68... | collective-permute-start | bytes 3145736 | tf_op jit(solution)/shard_map/ppermute | solution.py:46
  13.6 2.8 %collective-permute-start.3 = (f32[512,512]{1,0:T(8,128)S(1)}, f32[512,512]{1,0:T(8,128)}, u32[]{:S(2)}, u32[]{:S(2)}) collective-permute-start(f32[512,512]{1,0:T(8,128)S(1)} %get-tuple-element.28), channel_id=1, source_target_pairs={{0,64},{64,0},{1,65},{65,1},{2,66},{66,2},{3,67},{67,3},{4,68},{68... | collective-permute-start | bytes 3145736 | tf_op jit(solution)/shard_map/ppermute | solution.py:46
  16.4 0.7 broadcast_in_dim.22
  17.1 7.1 %all-to-all-start.1 = ((f32[4,2,2,8,512]{4,3,2,1,0:T(8,128)}), f32[4,2,2,8,512]{4,3,2,1,0:T(8,128)S(1)}, u32[]{:S(2)}, u32[]{:S(2)}) async-start(f32[4,2,2,8,512]{4,3,2,1,0:T(8,128)} %broadcast_in_dim.22), calls=%async_computation.1 | async-start | bytes 524288 | tf_op jit(solution)/shard_map/all_to_all | solution.py:150
  24.2 1.9 %collective-permute-start.1 = (f32[2,2,8,512]{3,2,1,0:T(8,128)S(1)}, f32[2,2,8,512]{3,2,1,0:T(8,128)S(1)}, u32[]{:S(2)}, u32[]{:S(2)}) collective-permute-start(f32[2,2,8,512]{3,2,1,0:T(8,128)S(1)} %get-tuple-element.25), channel_id=1, source_target_pairs={{0,1},{1,0},{2,3},{3,2},{4,5},{5,4},{6,7},{7,6},{8,9},{9,8},{10,11... | collective-permute-start | bytes 196616 | tf_op jit(solution)/shard_map/ppermute | solution.py:152
  26.1 1.2 collective-permute-done.1
  27.3 6.6 %all-to-all-done.1 = f32[4,2,2,8,512]{4,3,2,1,0:T(8,128)S(1)} async-done(((f32[4,2,2,8,512]{4,3,2,1,0:T(8,128)}), f32[4,2,2,8,512]{4,3,2,1,0:T(8,128)S(1)}, u32[]{:S(2)}, u32[]{:S(2)}) %all-to-all-start.1) | async-done | bytes 262176 | tf_op jit(solution)/shard_map/all_to_all | solution.py:150
  33.9 1.6 %broadcast_in_dim.23 = f32[8,4,2,2,8,512]{5,4,3,2,1,0:T(8,128)} broadcast(f32[4,2,2,8,512]{4,3,2,1,0:T(8,128)S(1)} %all-to-all-done.1), dimensions={1,2,3,4,5} | broadcast | bytes 2359296 | tf_op jit(solution)/shard_map/broadcast_in_dim | solution.py:155
  35.5 29.0 %conditional.1 = (f32[8,4,2,2,8,512]{5,4,3,2,1,0:T(8,128)}) conditional(s32[]{:T(128)} %convert_element_type.3, f32[8,4,2,2,8,512]{5,4,3,2,1,0:T(8,128)} %broadcast_in_dim.23, f32[8,4,2,2,8,512]{5,4,3,2,1,0:T(8,128)} %broadcast_in_dim.23), branch_computations={%region_0.1_spmd, %region_1.2_spmd} | conditional | bytes 12582948 | solution.py:156
  35.5 1.7 %copy-done.7 = f32[8,4,2,2,8,512]{5,4,3,2,1,0:T(8,128)S(1)} copy-done((f32[8,4,2,2,8,512]{5,4,3,2,1,0:T(8,128)S(1)}, f32[8,4,2,2,8,512]{5,4,3,2,1,0:T(8,128)}, u32[]{:S(2)}) %copy-start.7) | copy-done | bytes 2097176 | tf_op jit(solution)/shard_map/cond
  37.2 27.3 %all_to_all.24 = f32[8,4,2,2,8,512]{5,4,3,2,1,0:T(8,128)} all-to-all(f32[8,4,2,2,8,512]{5,4,3,2,1,0:T(8,128)S(1)} %copy-done.7), channel_id=1, replica_groups=mesh['x'=4,'zl'=2,'yh'=4,'yl'=2,'zh'=4,'c'=2] {'x','yl'}, dimensions={0} | all-to-all | bytes 4194304 | tf_op jit(solution)/shard_map/cond/branch_1_fun/all_to_all | solution.py:158
  64.5 6.6 %products.3 = f32[4,2,2,4,8,512]{5,4,3,2,1,0:T(8,128)} custom-call(s32[1]{0:T(128)} %bitcast.2.mine_ref, f32[4,2,4,2,2,8,512]{6,5,4,3,2,1,0:T(8,128)} %bitcast.16, f32[1,2,512,512]{3,2,1,0:T(8,128)S(1)} %copy-done.1, f32[1,2,512,512]{3,2,1,0:T(8,128)} %r_ref.3, f32[512,512]{1,0:T(8,128)} %collective-permute-done.2.l_in_ref, ...), custom_call_target="tpu_custom_call" | custom-call | flops 3221225472 | bytes 8388608 | tf_op jit(solution)/shard_map/products/pallas_call | solution.py:166
  71.1 5.2 %all-to-all-start.3 = ((f32[8,8,8,512]{3,2,1,0:T(8,128)}), f32[8,8,8,512]{3,2,1,0:T(8,128)S(1)}, u32[]{:S(2)}, u32[]{:S(2)}) async-start(f32[8,8,8,512]{3,2,1,0:T(8,128)} %bitcast.9), calls=%async_computation.3 | async-start | bytes 2097152 | tf_op jit(solution)/shard_map/all_to_all | solution.py:209
  76.4 6.6 %products.2 = f32[4,2,2,4,8,512]{5,4,3,2,1,0:T(8,128)} custom-call(s32[1]{0:T(128)} %bitcast.2.mine_ref, f32[4,2,4,2,2,8,512]{6,5,4,3,2,1,0:T(8,128)} %bitcast.17, f32[1,2,512,512]{3,2,1,0:T(8,128)S(1)} %copy-done.1, f32[1,2,512,512]{3,2,1,0:T(8,128)} %r_ref.3, f32[512,512]{1,0:T(8,128)} %collective-permute-done.2.l_in_ref, ...), custom_call_target="tpu_custom_call" | custom-call | flops 3221225472 | bytes 8388608 | tf_op jit(solution)/shard_map/products/pallas_call | solution.py:166
  83.0 3.3 %all-to-all-done.3.two_ref = f32[8,8,8,512]{3,2,1,0:T(8,128)S(1)} async-done(((f32[8,8,8,512]{3,2,1,0:T(8,128)}), f32[8,8,8,512]{3,2,1,0:T(8,128)S(1)}, u32[]{:S(2)}, u32[]{:S(2)}) %all-to-all-start.3) | async-done | bytes 1048608 | tf_op jit(solution)/shard_map/all_to_all | solution.py:209
  86.3 5.9 %all-to-all-start.2 = ((f32[8,8,8,512]{3,2,1,0:T(8,128)}), f32[8,8,8,512]{3,2,1,0:T(8,128)S(1)}, u32[]{:S(2)}, u32[]{:S(2)}) async-start(f32[8,8,8,512]{3,2,1,0:T(8,128)} %bitcast.8), calls=%async_computation.2 | async-start | bytes 2097152 | tf_op jit(solution)/shard_map/all_to_all | solution.py:209
  92.2 10.0 %collective-permute-start.5 = (f32[2,2,2,8,512]{4,3,2,1,0:T(8,128)S(1)}, f32[2,2,2,8,512]{4,3,2,1,0:T(8,128)S(1)}, u32[]{:S(2)}, u32[]{:S(2)}) collective-permute-start(f32[2,2,2,8,512]{4,3,2,1,0:T(8,128)S(1)} %pad_maximum_fusion.refs_0_), channel_id=1, source_target_pairs={{4,0},{6,2},{0,4},{2,6},{5,1},{7,3},{1,5},{3,7},{12,8},{14,10},{8,... | collective-permute-start | bytes 393224 | tf_op jit(solution)/shard_map/ppermute | solution.py:214
  102.2 1.9 %collective-permute-start.4 = (f32[2,2,2,8,512]{4,3,2,1,0:T(8,128)S(1)}, f32[2,2,2,8,512]{4,3,2,1,0:T(8,128)S(1)}, u32[]{:S(2)}, u32[]{:S(2)}) collective-permute-start(f32[2,2,2,8,512]{4,3,2,1,0:T(8,128)S(1)} %pad_maximum_fusion.refs_0_), channel_id=1, source_target_pairs={{2,0},{4,2},{6,4},{0,6},{3,1},{5,3},{7,5},{1,7},{10,8},{12,10},{14... | collective-permute-start | bytes 393224 | tf_op jit(solution)/shard_map/ppermute | solution.py:214
  104.2 0.8 near_sum.1
  105.0 1.2 collective-permute-done.5.refs_2_
  106.1 5.0 %collective-permute-done.4.refs_1_ = f32[2,2,2,8,512]{4,3,2,1,0:T(8,128)S(1)} collective-permute-done((f32[2,2,2,8,512]{4,3,2,1,0:T(8,128)S(1)}, f32[2,2,2,8,512]{4,3,2,1,0:T(8,128)S(1)}, u32[]{:S(2)}, u32[]{:S(2)}) %collective-permute-start.4) | collective-permute-done | bytes 131104 | tf_op jit(solution)/shard_map/ppermute | solution.py:214
  111.1 4.9 %all-to-all-start.4 = ((f32[8,2,8,512]{3,2,1,0:T(8,128)}), f32[8,2,8,512]{3,2,1,0:T(8,128)S(1)}, u32[]{:S(2)}, u32[]{:S(2)}) async-start(f32[8,2,8,512]{3,2,1,0:T(8,128)} %near_sum.1), calls=%async_computation.4 | async-start | bytes 524288 | tf_op jit(solution)/shard_map/all_to_all | solution.py:226
  116.0 5.2 %collective-permute-start.6 = (f32[2,2,2,8,512]{4,3,2,1,0:T(8,128)S(1)}, f32[2,2,2,8,512]{4,3,2,1,0:T(8,128)S(1)}, u32[]{:S(2)}, u32[]{:S(2)}) collective-permute-start(f32[2,2,2,8,512]{4,3,2,1,0:T(8,128)S(1)} %pad_maximum_fusion.refs_0_), channel_id=1, source_target_pairs={{6,0},{0,2},{2,4},{4,6},{7,1},{1,3},{3,5},{5,7},{14,8},{8,10},{10,... | collective-permute-start | bytes 393224 | tf_op jit(solution)/shard_map/ppermute | solution.py:214
  121.2 6.3 %collective-permute-done.6.refs_3_ = f32[2,2,2,8,512]{4,3,2,1,0:T(8,128)S(1)} collective-permute-done((f32[2,2,2,8,512]{4,3,2,1,0:T(8,128)S(1)}, f32[2,2,2,8,512]{4,3,2,1,0:T(8,128)S(1)}, u32[]{:S(2)}, u32[]{:S(2)}) %collective-permute-start.6) | collective-permute-done | bytes 131104 | tf_op jit(solution)/shard_map/ppermute | solution.py:214
  127.5 1.6 %copy-done = f32[2,512,512]{2,1,0:T(8,128)S(1)} copy-done((f32[2,512,512]{2,1,0:T(8,128)S(1)}, f32[2,512,512]{2,1,0:T(8,128)}, u32[]{:S(2)}) %copy-start) | copy-done | bytes 2097176
  129.1 1.5 %shift.1.shifted_ref = f32[2,2,8,512]{3,2,1,0:T(8,128)S(1)} custom-call(s32[2]{0:T(128)S(1)} %pad_add_fusion.place_ref, s32[16]{0:T(128)S(1)} %copy-done.6, f32[2,2,2,8,512]{4,3,2,1,0:T(8,128)S(1)} %pad_maximum_fusion.refs_0_, f32[2,2,2,8,512]{4,3,2,1,0:T(8,128)S(1)} %collective-permute-done.4.refs_1_, ...), custom_call_target="tpu_custom_call" | custom-call | flops 50331648 | bytes 3145728 | tf_op jit(solution)/shard_map/shift/pallas_call | solution.py:228
  130.6 1.2 finish.1
  (20 shorter events, 0.7 us)
Async XLA Ops:
  0.7 0.8 copy-start.2
  1.5 0.8 copy-start.3
  2.2 0.7 copy-start.4
  3.5 7.0 %collective-permute-start = (f32[2,8,512]{2,1,0:T(8,128)S(1)}, f32[2,8,512]{2,1,0:T(8,128)S(1)}, u32[]{:S(2)}, u32[]{:S(2)}) collective-permute-start(f32[2,8,512]{2,1,0:T(8,128)S(1)} %get-tuple-element.23), channel_id=1, source_target_pairs={{0,64},{64,0},{1,65},{65,1},{2,66},{66,2},{3,67},{67,3},{4,68},{68... | collective-permute-start | bytes 98312 | tf_op jit(solution)/shard_map/ppermute | solution.py:46
  10.5 54.0 %collective-permute-start.2 = (f32[512,512]{1,0:T(8,128)}, f32[512,512]{1,0:T(8,128)}, u32[]{:S(2)}, u32[]{:S(2)}) collective-permute-start(f32[512,512]{1,0:T(8,128)} %get-tuple-element.27), channel_id=1, source_target_pairs={{0,64},{64,0},{1,65},{65,1},{2,66},{66,2},{3,67},{67,3},{4,68},{68... | collective-permute-start | bytes 3145736 | tf_op jit(solution)/shard_map/ppermute | solution.py:46
  13.6 51.0 %collective-permute-start.3 = (f32[512,512]{1,0:T(8,128)S(1)}, f32[512,512]{1,0:T(8,128)}, u32[]{:S(2)}, u32[]{:S(2)}) collective-permute-start(f32[512,512]{1,0:T(8,128)S(1)} %get-tuple-element.28), channel_id=1, source_target_pairs={{0,64},{64,0},{1,65},{65,1},{2,66},{66,2},{3,67},{67,3},{4,68},{68... | collective-permute-start | bytes 3145736 | tf_op jit(solution)/shard_map/ppermute | solution.py:46
  17.1 16.8 %all-to-all-start.1 = ((f32[4,2,2,8,512]{4,3,2,1,0:T(8,128)}), f32[4,2,2,8,512]{4,3,2,1,0:T(8,128)S(1)}, u32[]{:S(2)}, u32[]{:S(2)}) async-start(f32[4,2,2,8,512]{4,3,2,1,0:T(8,128)} %broadcast_in_dim.22), calls=%async_computation.1 | async-start | bytes 524288 | tf_op jit(solution)/shard_map/all_to_all | solution.py:150
  24.2 3.1 %collective-permute-start.1 = (f32[2,2,8,512]{3,2,1,0:T(8,128)S(1)}, f32[2,2,8,512]{3,2,1,0:T(8,128)S(1)}, u32[]{:S(2)}, u32[]{:S(2)}) collective-permute-start(f32[2,2,8,512]{3,2,1,0:T(8,128)S(1)} %get-tuple-element.25), channel_id=1, source_target_pairs={{0,1},{1,0},{2,3},{3,2},{4,5},{5,4},{6,7},{7,6},{8,9},{9,8},{10,11... | collective-permute-start | bytes 196616 | tf_op jit(solution)/shard_map/ppermute | solution.py:152
  35.5 29.0 %copy-start.1 = (f32[1,2,512,512]{3,2,1,0:T(8,128)S(1)}, f32[1,2,512,512]{3,2,1,0:T(8,128)}, u32[]{:S(2)}) copy-start(f32[1,2,512,512]{3,2,1,0:T(8,128)} %l_ref.3) | copy-start | bytes 6291460
  35.5 1.7 %copy-start.7 = (f32[8,4,2,2,8,512]{5,4,3,2,1,0:T(8,128)S(1)}, f32[8,4,2,2,8,512]{5,4,3,2,1,0:T(8,128)}, u32[]{:S(2)}) copy-start(f32[8,4,2,2,8,512]{5,4,3,2,1,0:T(8,128)} %param.1) | copy-start | bytes 6291460 | tf_op jit(solution)/shard_map/cond
  71.1 15.2 %all-to-all-start.3 = ((f32[8,8,8,512]{3,2,1,0:T(8,128)}), f32[8,8,8,512]{3,2,1,0:T(8,128)S(1)}, u32[]{:S(2)}, u32[]{:S(2)}) async-start(f32[8,8,8,512]{3,2,1,0:T(8,128)} %bitcast.9), calls=%async_computation.3 | async-start | bytes 2097152 | tf_op jit(solution)/shard_map/all_to_all | solution.py:209
  86.3 17.9 %all-to-all-start.2 = ((f32[8,8,8,512]{3,2,1,0:T(8,128)}), f32[8,8,8,512]{3,2,1,0:T(8,128)S(1)}, u32[]{:S(2)}, u32[]{:S(2)}) async-start(f32[8,8,8,512]{3,2,1,0:T(8,128)} %bitcast.8), calls=%async_computation.2 | async-start | bytes 2097152 | tf_op jit(solution)/shard_map/all_to_all | solution.py:209
  92.2 35.4 %copy-start.6 = (s32[16]{0:T(128)S(1)}, s32[16]{0:T(128)}, u32[]{:S(2)}) copy-start(s32[16]{0:T(128)} %pair_ref.1) | copy-start | bytes 196
  92.2 14.0 %collective-permute-start.5 = (f32[2,2,2,8,512]{4,3,2,1,0:T(8,128)S(1)}, f32[2,2,2,8,512]{4,3,2,1,0:T(8,128)S(1)}, u32[]{:S(2)}, u32[]{:S(2)}) collective-permute-start(f32[2,2,2,8,512]{4,3,2,1,0:T(8,128)S(1)} %pad_maximum_fusion.refs_0_), channel_id=1, source_target_pairs={{4,0},{6,2},{0,4},{2,6},{5,1},{7,3},{1,5},{3,7},{12,8},{14,10},{8,... | collective-permute-start | bytes 393224 | tf_op jit(solution)/shard_map/ppermute | solution.py:214
  102.2 8.9 %collective-permute-start.4 = (f32[2,2,2,8,512]{4,3,2,1,0:T(8,128)S(1)}, f32[2,2,2,8,512]{4,3,2,1,0:T(8,128)S(1)}, u32[]{:S(2)}, u32[]{:S(2)}) collective-permute-start(f32[2,2,2,8,512]{4,3,2,1,0:T(8,128)S(1)} %pad_maximum_fusion.refs_0_), channel_id=1, source_target_pairs={{2,0},{4,2},{6,4},{0,6},{3,1},{5,3},{7,5},{1,7},{10,8},{12,10},{14... | collective-permute-start | bytes 393224 | tf_op jit(solution)/shard_map/ppermute | solution.py:214
  105.0 25.6 %copy-start.5 = (s32[16]{0:T(128)S(1)}, s32[16]{0:T(128)}, u32[]{:S(2)}) copy-start(s32[16]{0:T(128)} %dims_ref.3) | copy-start | bytes 196
  111.1 19.5 %all-to-all-start.4 = ((f32[8,2,8,512]{3,2,1,0:T(8,128)}), f32[8,2,8,512]{3,2,1,0:T(8,128)S(1)}, u32[]{:S(2)}, u32[]{:S(2)}) async-start(f32[8,2,8,512]{3,2,1,0:T(8,128)} %near_sum.1), calls=%async_computation.4 | async-start | bytes 524288 | tf_op jit(solution)/shard_map/all_to_all | solution.py:226
  116.0 11.6 %collective-permute-start.6 = (f32[2,2,2,8,512]{4,3,2,1,0:T(8,128)S(1)}, f32[2,2,2,8,512]{4,3,2,1,0:T(8,128)S(1)}, u32[]{:S(2)}, u32[]{:S(2)}) collective-permute-start(f32[2,2,2,8,512]{4,3,2,1,0:T(8,128)S(1)} %pad_maximum_fusion.refs_0_), channel_id=1, source_target_pairs={{6,0},{0,2},{2,4},{4,6},{7,1},{1,3},{3,5},{5,7},{14,8},{8,10},{10,... | collective-permute-start | bytes 393224 | tf_op jit(solution)/shard_map/ppermute | solution.py:214
  127.5 1.6 %copy-start = (f32[2,512,512]{2,1,0:T(8,128)S(1)}, f32[2,512,512]{2,1,0:T(8,128)}, u32[]{:S(2)}) copy-start(f32[2,512,512]{2,1,0:T(8,128)} %refs_4_.1) | copy-start | bytes 6291460

commit v3 on v2

v3 whole, which is shorter than its diff:
```python
import functools

import jax
import jax.numpy as jnp
from jax import lax
from jax.experimental import pallas as pl
from jax.experimental.pallas import tpu as pltpu
from jax.sharding import Mesh, PartitionSpec as P

AXES = ("x", "zl", "yh", "yl", "zh", "c")
SIZES = (4, 2, 4, 2, 4, 2)
OPS = ("x", "zl", "yh", "yl")
WF = ("zh", "c")
FAR = ("zl", "yh")
NEAR = ("x", "yl")
F32 = jnp.float32
BF16 = jnp.bfloat16
VMEM = pl.BlockSpec(memory_space=pltpu.VMEM)
SMEM = pl.BlockSpec(memory_space=pltpu.SMEM)
HBM = pl.BlockSpec(memory_space=pl.ANY)
PARAMS = pltpu.CompilerParams(vmem_limit_bytes=48 * 1024 * 1024)
WIDE = pltpu.CompilerParams(vmem_limit_bytes=60 * 1024 * 1024)


def shape(*dims):
    return jax.ShapeDtypeStruct(dims, F32)


def halves(value):
    high = value.astype(BF16)
    return high, (value - high.astype(F32)).astype(BF16)


def times(a, b):
    return jnp.dot(a, b, preferred_element_type=F32)


def times_t(a, b):
    return lax.dot_general(a, b, (((1,), (1,)), ((), ())), preferred_element_type=F32)


def live_mask(place, place_ref, dims_ref, block, rows, width):
    size = dims_ref[place_ref[1] * 2 + block]
    row = place * rows + lax.broadcasted_iota(jnp.int32, (rows, width), 0)
    column = lax.broadcasted_iota(jnp.int32, (rows, width), 1)
    return (row < size) & (column < size)


def swap(value):
    return lax.ppermute(value, "zl", [(0, 1), (1, 0)])


def after(value, earlier):
    return lax.optimization_barrier((value, earlier))[0]


def pick_kernel(spot_ref, left_ref, right_ref, out_ref, held, in_sems, out_sems):
    quarter = held.shape[1] // 4
    pieces = [(side, pl.ds(i * quarter, quarter)) for side in range(2) for i in range(4)]
    ins, outs = [], []
    for at, (side, rows) in enumerate(pieces):
        source = (left_ref, right_ref)[side].at[0, 1 - spot_ref[0], rows]
        ins.append(pltpu.make_async_copy(source, held.at[side, rows], in_sems.at[at]))
        outs.append(
            pltpu.make_async_copy(held.at[side, rows], out_ref.at[side, rows], out_sems.at[at])
        )
    for copy in ins:
        copy.start()
    for copy_in, copy_out in zip(ins, outs):
        copy_in.wait()
        copy_out.start()
    for copy in outs:
        copy.wait()


def spread_kernel(place_ref, dims_ref, one_ref, two_ref, got_ref, far_ref, live_ref):
    blocks, rows, width = one_ref.shape
    mine = place_ref[0] // 8 % 2
    for block in range(blocks):
        mask = live_mask(place_ref[0], place_ref, dims_ref, block, rows, width)
        for vector, ref in enumerate((one_ref, two_ref)):
            live_ref[block, vector] = jnp.where(mask, ref[block], 0.0)
    neighbour = place_ref[0] + 8 - 16 * mine
    mask = live_mask(neighbour, place_ref, dims_ref, mine, rows, width)
    for vector in range(2):
        own = live_ref[mine, vector]
        got = jnp.where(mask, got_ref[vector], 0.0)
        for slot in range(4):
            far_ref[slot, 0, vector] = own
            far_ref[slot, 1, vector] = got


def product_kernel(
    vector, spot_ref, g_ref, l_ref, r_ref, pair_ref, out_ref,
    g, ops, out, ph, pw, mh, ml, rh, rl, sems, out_sems,
):
    width = g.shape[-1]
    half = width // 2
    sources = (l_ref.at[0, spot_ref[0]], pair_ref.at[0], r_ref.at[0, spot_ref[0]], pair_ref.at[1])
    loads = [pltpu.make_async_copy(g_ref.at[:, :, :, :, vector], g, sems.at[4])] + [
        pltpu.make_async_copy(source, ops.at[at], sems.at[at]) for at, source in enumerate(sources)
    ]
    for load in loads:
        load.start()
    loads[0].wait()
    for x in range(4):
        for z in range(2):
            part = g[x, :, :, (z + spot_ref[0]) % 2].transpose(1, 0, 2, 3).reshape(64, width)
            rows = pl.ds(x * 128 + z * 64, 64)
            ph[rows], pw[rows] = halves(part)
    for t in range(2):
        loads[1 + t].wait()
        for i in range(2):
            rows = pl.ds(i * half, half)
            high, low = halves(ops[t, rows])
            m = times(high, ph[...]) + times(low, ph[...]) + times(high, pw[...])
            mh[t, rows], ml[t, rows] = halves(m)
    for t in range(2):
        loads[3 + t].wait()
        rh[t], rl[t] = halves(ops[2 + t])
    stores = []
    for i in range(2):
        rows = pl.ds(i * half, half)
        s = times_t(mh[0, rows], rh[0]) + times_t(ml[0, rows], rh[0]) + times_t(mh[0, rows], rl[0])
        s += times_t(mh[1, rows], rh[1]) + times_t(ml[1, rows], rh[1]) + times_t(mh[1, rows], rl[1])
        s = s.reshape(2, 2, 4, 2, 8, width).transpose(0, 3, 1, 2, 4, 5)
        out[pl.ds(i * 2, 2)] = s
        place = pl.ds(i * 2, 2)
        stores.append(pltpu.make_async_copy(out.at[place], out_ref.at[place], out_sems.at[i]))
        stores[-1].start()
    for store in stores:
        store.wait()


def sum_kernel(one_ref, two_ref, out_ref):
    for vector, ref in enumerate((one_ref, two_ref)):
        total = ref[0]
        for source in range(1, ref.shape[0]):
            total = total + ref[source]
        out_ref[:, vector] = total


def held_rows(place_ref, pair, chip_ref, next_ref):
    wf, core = place_ref[1], (pair // 2 + place_ref[1]) % 2
    here = (pair // 4 + wf // 2) % 2 == 0
    return jnp.where(here, chip_ref[core, pair % 2], next_ref[core, pair % 2])


def choose_kernel(place_ref, pair_ref, chip_ref, next_ref, out_ref):
    far_wf = (place_ref[1] + 4) % 8
    for block in range(out_ref.shape[0]):
        out_ref[block] = held_rows(place_ref, pair_ref[far_wf * 2 + block], chip_ref, next_ref)


def shift_kernel(place_ref, pair_ref, chip_ref, next_ref, far_ref, shift_ref, out_ref):
    blocks, width = shift_ref.shape[0], shift_ref.shape[-1]
    for block in range(blocks):
        pair = pair_ref[place_ref[1] * 2 + block]
        held = pair // 8 == place_ref[1] // 4
        paired = jnp.where(held, held_rows(place_ref, pair, chip_ref, next_ref), far_ref[block])
        high, low = halves(paired.reshape(16, width))
        s_high, s_low = halves(shift_ref[block])
        out = times_t(high, s_high) + times_t(low, s_high) + times_t(high, s_low)
        out_ref[block] = out.reshape(2, 8, width)


def final_kernel(place_ref, dims_ref, back_ref, shifted_ref, one_ref, two_ref):
    blocks, rows, width = one_ref.shape
    for block in range(blocks):
        mask = live_mask(place_ref[0], place_ref, dims_ref, block, rows, width)
        for vector, ref in enumerate((one_ref, two_ref)):
            total = shifted_ref[block, vector]
            for source in range(4):
                total = total + back_ref[block * 4 + source, vector]
            ref[block] = jnp.where(mask, total, 0.0)


def per_device(psi_one, psi_two, left_ops, right_ops, shift_ops, block_dims, partner):
    blocks, rows, width = psi_one.shape
    place = jnp.stack([lax.axis_index(OPS), lax.axis_index(WF)]).astype(jnp.int32)

    mine = lax.axis_index("zl").astype(jnp.int32)
    spot = mine[None]
    got = swap(
        jnp.stack(
            [lax.dynamic_index_in_dim(psi, 1 - mine, 0, False) for psi in (psi_one, psi_two)]
        )
    )
    pair_out = pl.pallas_call(
        pick_kernel,
        out_shape=shape(2, width, width),
        in_specs=[SMEM, HBM, HBM],
        out_specs=HBM,
        scratch_shapes=[
            pltpu.VMEM((2, width, width), F32),
            pltpu.SemaphoreType.DMA((8,)),
            pltpu.SemaphoreType.DMA((8,)),
        ],
        compiler_params=WIDE,
        name="pick",
    )(spot, left_ops, right_ops)
    got, pair_out = lax.optimization_barrier((got, pair_out))
    pair_in = swap(pair_out)

    far_out, live = pl.pallas_call(
        spread_kernel,
        out_shape=(shape(4, 2, 2, rows, width), shape(blocks, 2, rows, width)),
        in_specs=[SMEM, SMEM, VMEM, VMEM, VMEM],
        out_specs=(VMEM, VMEM),
        compiler_params=PARAMS,
        name="spread",
    )(place, block_dims, psi_one, psi_two, got)
    far_in = lax.all_to_all(far_out, "yh", 0, 0, tiled=True)

    other_core = lax.ppermute(live, "c", [(0, 1), (1, 0)])
    far_in, other_core = lax.optimization_barrier((far_in, other_core))

    near_in = lax.cond(
        lax.optimization_barrier(jnp.bool_(True)),
        lambda value: lax.all_to_all(
            jnp.broadcast_to(value[None], (8,) + value.shape), NEAR, 0, 0, tiled=True
        ),
        lambda value: jnp.zeros((8,) + value.shape, F32),
        far_in,
    )
    near_in, pair_in = lax.optimization_barrier((near_in, pair_in))

    products = []
    for vector in range(2):
        sums = pl.pallas_call(
            functools.partial(product_kernel, vector),
            out_shape=shape(4, 2, 2, 4, rows, width),
            in_specs=[SMEM, HBM, HBM, HBM, HBM],
            out_specs=HBM,
            scratch_shapes=[
                pltpu.VMEM((4, 2, 4, 2, rows, width), F32),
                pltpu.VMEM((4, width, width), F32),
                pltpu.VMEM((4, 2, 2, 4, rows, width), F32),
                pltpu.VMEM((width, width), BF16),
                pltpu.VMEM((width, width), BF16),
                pltpu.VMEM((2, width, width), BF16),
                pltpu.VMEM((2, width, width), BF16),
                pltpu.VMEM((2, width, width), BF16),
                pltpu.VMEM((2, width, width), BF16),
                pltpu.SemaphoreType.DMA((5,)),
                pltpu.SemaphoreType.DMA((2,)),
            ],
            compiler_params=WIDE,
            cost_estimate=pl.CostEstimate(
                flops=12 * 2 * 512**3, bytes_accessed=8 * 2**20, transcendentals=0
            ),
            name="products",
        )(spot, near_in.reshape(4, 2, 4, 2, 2, rows, width), left_ops, right_ops, pair_in)
        products.append(sums.reshape(8, 8, rows, width))

    chip = after(jnp.stack([live, other_core]), near_in)
    next_chip = lax.ppermute(chip, "zh", [(0, 1), (1, 0), (2, 3), (3, 2)])

    near_back_one = lax.all_to_all(products[0], NEAR, 0, 0, tiled=True)
    products[1], next_chip = lax.optimization_barrier((products[1], next_chip))
    near_backs = [near_back_one, lax.all_to_all(products[1], NEAR, 0, 0, tiled=True)]
    near_sum = pl.pallas_call(
        sum_kernel,
        out_shape=shape(8, 2, rows, width),
        in_specs=[VMEM, VMEM],
        out_specs=VMEM,
        compiler_params=PARAMS,
        name="near_sum",
    )(*near_backs)
    chosen = pl.pallas_call(
        choose_kernel,
        out_shape=shape(blocks, 2, rows, width),
        in_specs=[SMEM, SMEM, VMEM, VMEM],
        out_specs=VMEM,
        compiler_params=PARAMS,
        name="choose",
    )(place, partner, chip, next_chip)
    from_far = lax.ppermute(chosen, "zh", [(0, 2), (2, 0), (1, 3), (3, 1)])
    near_sum, from_far = lax.optimization_barrier((near_sum, from_far))
    far_back = lax.all_to_all(near_sum, FAR, 0, 0, tiled=True)

    shifted = pl.pallas_call(
        shift_kernel,
        out_shape=shape(blocks, 2, rows, width),
        in_specs=[SMEM, SMEM] + [VMEM] * 4,
        out_specs=VMEM,
        compiler_params=PARAMS,
        cost_estimate=pl.CostEstimate(
            flops=3 * 2 * 32 * 512**2, bytes_accessed=3 * 2**20, transcendentals=0
        ),
        name="shift",
    )(place, partner, chip, next_chip, from_far, shift_ops)

    return pl.pallas_call(
        final_kernel,
        out_shape=(shape(blocks, rows, width), shape(blocks, rows, width)),
        in_specs=[SMEM, SMEM, VMEM, VMEM],
        out_specs=(VMEM, VMEM),
        compiler_params=PARAMS,
        name="finish",
    )(place, block_dims, far_back, shifted)


def solution(mesh):
    fine = Mesh(mesh.devices.reshape(SIZES), AXES)
    in_specs = (
        P(WF, OPS, None),
        P(WF, OPS, None),
        P(OPS, WF, None, None),
        P(OPS, WF, None, None),
        P(WF, None, None),
        P(),
        P(),
    )
    out_specs = (P(WF, OPS, None), P(WF, OPS, None))
    return jax.shard_map(
        per_device, mesh=fine, in_specs=in_specs, out_specs=out_specs, check_vma=False
    )
```

time: 133 us -> 119 us (0.89)
  the two profiles are of different devices: /device:TPU:2 before, /device:TPU:10 now
where the time goes in v3:
time: 119 us
  starting transfers between devices  49.3 us (41%)
  blocking collectives  26.7 us (22%)
  Pallas kernels  20.1 us (17%)
  waiting for transfers between devices  18.8 us (16%)
  local copies, waits for them, and re-layouts  2.61 us (2%)
    all_to_all x1, blocking collectives, per_device(): lax.all_to_all(jnp.broadcast_to(value[None], (8,) + value.shape), NEAR, 0...  26.7 us
    pallas_call x2, Pallas kernels, per_device(): pl.pallas_call(functools.partial(product_kernel, vector), out_shape=shape...  12.4 us
    ppermute x1, starting transfers between devices, per_device(): from_far = lax.ppermute(chosen, 'zh', [(0, 2), (2, 0), (1, 3), (3, 1)])  10 us
    all_to_all x1, waiting for transfers between devices, per_device(): far_back = lax.all_to_all(near_sum, FAR, 0, 0, tiled=True)  7.61 us
    ppermute x2, starting transfers between devices, swap(): return lax.ppermute(value, 'zl', [(0, 1), (1, 0)])  7.59 us
    all_to_all x1, waiting for transfers between devices, per_device(): far_in = lax.all_to_all(far_out, 'yh', 0, 0, tiled=True)  6.96 us
    all_to_all x1, starting transfers between devices, per_device(): far_back = lax.all_to_all(near_sum, FAR, 0, 0, tiled=True)  6.2 us
    all_to_all x1, starting transfers between devices, per_device(): far_in = lax.all_to_all(far_out, 'yh', 0, 0, tiled=True)  6.19 us
  transfers between devices with their start and end apart: 9, of which 7 were waited for; matrix products, arithmetic and copies ran while one was open for 0% of the time, Pallas kernels for 11%

profile of v3, /device:TPU:10, one launch (start us, length us, event | category | flops | bytes accessed | tf_op | source)
XLA Modules:
  0.0 118.5 jit_solution(2439194958474869924)
XLA Ops:
  0.6 0.7 constant_dynamic-slice_fusion
  1.4 4.3 %collective-permute-start = (f32[2,8,512]{2,1,0:T(8,128)S(1)}, f32[2,8,512]{2,1,0:T(8,128)S(1)}, u32[]{:S(2)}, u32[]{:S(2)}) collective-permute-start(f32[2,8,512]{2,1,0:T(8,128)S(1)} %pad_maximum_fusion.1), channel_id=1, source_target_pairs={{0,64},{64,0},{1,65},{65,1},{2,66},{66,2},{3,67},{67,3},{4,68},{68... | collective-permute-start | bytes 98312 | tf_op jit(solution)/shard_map/ppermute | solution.py:50
  5.7 0.0 copy-start.1
  5.7 0.0 copy-start.2
  5.7 2.4 %pick.1 = f32[2,512,512]{2,1,0:T(8,128)} custom-call(s32[1]{0:T(128)} %bitcast.2.spot_ref, f32[1,2,512,512]{3,2,1,0:T(8,128)} %l_ref.3, f32[1,2,512,512]{3,2,1,0:T(8,128)} %r_ref.3), custom_call_target="tpu_custom_call" | custom-call | tf_op jit(solution)/shard_map/pick/pallas_call | solution.py:189
  8.1 3.3 %collective-permute-start.2 = (f32[2,512,512]{2,1,0:T(8,128)}, f32[2,512,512]{2,1,0:T(8,128)}, u32[]{:S(2)}, u32[]{:S(2)}) collective-permute-start(f32[2,512,512]{2,1,0:T(8,128)} %pick.1), channel_id=1, source_target_pairs={{0,64},{64,0},{1,65},{65,1},{2,66},{66,2},{3,67},{67,3},{4,68},{68... | collective-permute-start | bytes 6291464 | tf_op jit(solution)/shard_map/ppermute | solution.py:50
  11.5 0.1 pad_add_fusion.place_ref
  11.6 1.3 %spread.1 = (f32[4,2,2,8,512]{4,3,2,1,0:T(8,128)}, f32[2,2,8,512]{3,2,1,0:T(8,128)S(1)}) custom-call(s32[2]{0:T(128)S(1)} %pad_add_fusion.place_ref, s32[16]{0:T(128)S(1)} %copy-done.4, f32[2,8,512]{2,1,0:T(8,128)S(1)} %copy-done.1, f32[2,8,512]{2,1,0:T(8,128)S(1)} %copy-done.2, f32[2,8,512]{2,1,0:T(8,128)S(1)} %collective-permute-done.got_ref), custom_call_target="tpu_custom_call" | custom-call | tf_op jit(solution)/shard_map/spread/pallas_call | solution.py:205
  12.9 6.2 %all-to-all-start.1 = ((f32[4,2,2,8,512]{4,3,2,1,0:T(8,128)}), f32[4,2,2,8,512]{4,3,2,1,0:T(8,128)S(1)}, u32[]{:S(2)}, u32[]{:S(2)}) async-start(f32[4,2,2,8,512]{4,3,2,1,0:T(8,128)} %get-tuple-element.20), calls=%async_computation.1 | async-start | bytes 524288 | tf_op jit(solution)/shard_map/all_to_all | solution.py:213
  19.1 1.9 %collective-permute-start.1 = (f32[2,2,8,512]{3,2,1,0:T(8,128)S(1)}, f32[2,2,8,512]{3,2,1,0:T(8,128)S(1)}, u32[]{:S(2)}, u32[]{:S(2)}) collective-permute-start(f32[2,2,8,512]{3,2,1,0:T(8,128)S(1)} %get-tuple-element.21), channel_id=1, source_target_pairs={{0,1},{1,0},{2,3},{3,2},{4,5},{5,4},{6,7},{7,6},{8,9},{9,8},{10,11... | collective-permute-start | bytes 196616 | tf_op jit(solution)/shard_map/ppermute | solution.py:215
  21.0 1.2 %collective-permute-done.1 = f32[2,2,8,512]{3,2,1,0:T(8,128)S(1)} collective-permute-done((f32[2,2,8,512]{3,2,1,0:T(8,128)S(1)}, f32[2,2,8,512]{3,2,1,0:T(8,128)S(1)}, u32[]{:S(2)}, u32[]{:S(2)}) %collective-permute-start.1) | collective-permute-done | bytes 65568 | tf_op jit(solution)/shard_map/ppermute | solution.py:215
  22.2 7.0 %all-to-all-done.1 = f32[4,2,2,8,512]{4,3,2,1,0:T(8,128)S(1)} async-done(((f32[4,2,2,8,512]{4,3,2,1,0:T(8,128)}), f32[4,2,2,8,512]{4,3,2,1,0:T(8,128)S(1)}, u32[]{:S(2)}, u32[]{:S(2)}) %all-to-all-start.1) | async-done | bytes 262176 | tf_op jit(solution)/shard_map/all_to_all | solution.py:213
  29.2 27.0 %conditional.1 = (f32[8,4,2,2,8,512]{5,4,3,2,1,0:T(8,128)S(1)}) conditional(s32[]{:T(128)} %convert_element_type.3, () %tuple.19, f32[4,2,2,8,512]{4,3,2,1,0:T(8,128)S(1)} %all-to-all-done.1), branch_computations={%region_0.1_spmd, %region_1.2_spmd} | conditional | bytes 6553608 | solution.py:218
  29.2 0.3 broadcast_in_dim.0
  29.4 26.7 %all_to_all.24 = f32[8,4,2,2,8,512]{5,4,3,2,1,0:T(8,128)S(1)} all-to-all(f32[8,4,2,2,8,512]{5,4,3,2,1,0:T(8,128)S(1)} %broadcast_in_dim.0), channel_id=1, replica_groups=mesh['x'=4,'zl'=2,'yh'=4,'yl'=2,'zh'=4,'c'=2] {'x','yl'}, dimensions={0} | all-to-all | bytes 4194304 | tf_op jit(solution)/shard_map/cond/branch_1_fun/all_to_all | solution.py:220
  56.2 1.3 %collective-permute-done.2.pair_ref = f32[2,512,512]{2,1,0:T(8,128)} collective-permute-done((f32[2,512,512]{2,1,0:T(8,128)}, f32[2,512,512]{2,1,0:T(8,128)}, u32[]{:S(2)}, u32[]{:S(2)}) %collective-permute-start.2) | collective-permute-done | bytes 2097184 | tf_op jit(solution)/shard_map/ppermute | solution.py:50
  57.4 6.2 %products.2 = f32[4,2,2,4,8,512]{5,4,3,2,1,0:T(8,128)} custom-call(s32[1]{0:T(128)} %bitcast.2.spot_ref, f32[4,2,4,2,2,8,512]{6,5,4,3,2,1,0:T(8,128)S(1)} %bitcast.9, f32[1,2,512,512]{3,2,1,0:T(8,128)} %l_ref.3, f32[1,2,512,512]{3,2,1,0:T(8,128)} %r_ref.3, f32[2,512,512]{2,1,0:T(8,128)} %collective-permute-done.2.pair_ref), custom_call_target="tpu_custom_call" | custom-call | flops 3221225472 | bytes 8388608 | tf_op jit(solution)/shard_map/products/pallas_call | solution.py:230
  63.6 5.7 %all-to-all-start.2 = ((f32[8,8,8,512]{3,2,1,0:T(8,128)}), f32[8,8,8,512]{3,2,1,0:T(8,128)S(1)}, u32[]{:S(2)}, u32[]{:S(2)}) async-start(f32[8,8,8,512]{3,2,1,0:T(8,128)} %bitcast.12), calls=%async_computation.2 | async-start | bytes 2097152 | tf_op jit(solution)/shard_map/all_to_all | solution.py:259
  69.4 6.1 %collective-permute-start.3 = (f32[2,2,2,8,512]{4,3,2,1,0:T(8,128)S(1)}, f32[2,2,2,8,512]{4,3,2,1,0:T(8,128)S(1)}, u32[]{:S(2)}, u32[]{:S(2)}) collective-permute-start(f32[2,2,2,8,512]{4,3,2,1,0:T(8,128)S(1)} %pad_maximum_fusion.chip_ref), channel_id=1, source_target_pairs={{0,2},{2,0},{4,6},{6,4},{1,3},{3,1},{5,7},{7,5},{8,10},{10,8},{12,... | collective-permute-start | bytes 393224 | tf_op jit(solution)/shard_map/ppermute | solution.py:257
  75.5 6.2 %products.3 = f32[4,2,2,4,8,512]{5,4,3,2,1,0:T(8,128)} custom-call(s32[1]{0:T(128)} %bitcast.2.spot_ref, f32[4,2,4,2,2,8,512]{6,5,4,3,2,1,0:T(8,128)S(1)} %bitcast.10, f32[1,2,512,512]{3,2,1,0:T(8,128)} %l_ref.3, f32[1,2,512,512]{3,2,1,0:T(8,128)} %r_ref.3, f32[2,512,512]{2,1,0:T(8,128)} %collective-permute-done.2.pair_ref), custom_call_target="tpu_custom_call" | custom-call | flops 3221225472 | bytes 8388608 | tf_op jit(solution)/shard_map/products/pallas_call | solution.py:230
  81.7 0.1 all-to-all-done.2.one_ref
  81.8 5.6 %all-to-all-start.3 = ((f32[8,8,8,512]{3,2,1,0:T(8,128)}), f32[8,8,8,512]{3,2,1,0:T(8,128)S(1)}, u32[]{:S(2)}, u32[]{:S(2)}) async-start(f32[8,8,8,512]{3,2,1,0:T(8,128)} %bitcast.11), calls=%async_computation.3 | async-start | bytes 2097152 | tf_op jit(solution)/shard_map/all_to_all | solution.py:261
  87.4 0.6 choose.1
  88.0 10.0 %collective-permute-start.4 = (f32[2,2,8,512]{3,2,1,0:T(8,128)S(1)}, f32[2,2,8,512]{3,2,1,0:T(8,128)S(1)}, u32[]{:S(2)}, u32[]{:S(2)}) collective-permute-start(f32[2,2,8,512]{3,2,1,0:T(8,128)S(1)} %choose.1), channel_id=1, source_target_pairs={{0,4},{4,0},{2,6},{6,2},{1,5},{5,1},{3,7},{7,3},{8,12},{12,8},{10,... | collective-permute-start | bytes 196616 | tf_op jit(solution)/shard_map/ppermute | solution.py:278
  98.0 1.0 all-to-all-done.3.two_ref
  99.0 0.8 near_sum.1
  99.8 0.7 collective-permute-done.4.far_ref
  100.5 6.2 %all-to-all-start.4 = ((f32[8,2,8,512]{3,2,1,0:T(8,128)}), f32[8,2,8,512]{3,2,1,0:T(8,128)S(1)}, u32[]{:S(2)}, u32[]{:S(2)}) async-start(f32[8,2,8,512]{3,2,1,0:T(8,128)} %near_sum.1), calls=%async_computation.4 | async-start | bytes 524288 | tf_op jit(solution)/shard_map/all_to_all | solution.py:280
  106.7 1.6 %copy-done = f32[2,512,512]{2,1,0:T(8,128)S(1)} copy-done((f32[2,512,512]{2,1,0:T(8,128)S(1)}, f32[2,512,512]{2,1,0:T(8,128)}, u32[]{:S(2)}) %copy-start) | copy-done | bytes 2097176
  108.3 1.5 %shift.1.shifted_ref = f32[2,2,8,512]{3,2,1,0:T(8,128)S(1)} custom-call(s32[2]{0:T(128)S(1)} %pad_add_fusion.place_ref, s32[16]{0:T(128)S(1)} %copy-done.3, f32[2,2,2,8,512]{4,3,2,1,0:T(8,128)S(1)} %pad_maximum_fusion.chip_ref, f32[2,2,2,8,512]{4,3,2,1,0:T(8,128)S(1)} %collective-permute-done.3.next_ref, ...), custom_call_target="tpu_custom_call" | custom-call | flops 50331648 | bytes 3145728 | tf_op jit(solution)/shard_map/shift/pallas_call | solution.py:282
  109.7 7.6 %all-to-all-done.4.back_ref = f32[8,2,8,512]{3,2,1,0:T(8,128)S(1)} async-done(((f32[8,2,8,512]{3,2,1,0:T(8,128)}), f32[8,2,8,512]{3,2,1,0:T(8,128)S(1)}, u32[]{:S(2)}, u32[]{:S(2)}) %all-to-all-start.4) | async-done | bytes 262176 | tf_op jit(solution)/shard_map/all_to_all | solution.py:280
  117.4 1.2 finish.1
  (11 shorter events, 0.0 us)
Async XLA Ops:
  1.4 6.7 %collective-permute-start = (f32[2,8,512]{2,1,0:T(8,128)S(1)}, f32[2,8,512]{2,1,0:T(8,128)S(1)}, u32[]{:S(2)}, u32[]{:S(2)}) collective-permute-start(f32[2,8,512]{2,1,0:T(8,128)S(1)} %pad_maximum_fusion.1), channel_id=1, source_target_pairs={{0,64},{64,0},{1,65},{65,1},{2,66},{66,2},{3,67},{67,3},{4,68},{68... | collective-permute-start | bytes 98312 | tf_op jit(solution)/shard_map/ppermute | solution.py:50
  5.7 5.9 %copy-start.1 = (f32[2,8,512]{2,1,0:T(8,128)S(1)}, f32[2,8,512]{2,1,0:T(8,128)}, u32[]{:S(2)}) copy-start(f32[2,8,512]{2,1,0:T(8,128)} %one_ref.1) | copy-start | bytes 98308
  5.7 5.9 %copy-start.2 = (f32[2,8,512]{2,1,0:T(8,128)S(1)}, f32[2,8,512]{2,1,0:T(8,128)}, u32[]{:S(2)}) copy-start(f32[2,8,512]{2,1,0:T(8,128)} %two_ref.1) | copy-start | bytes 98308
  5.7 5.9 %copy-start.4 = (s32[16]{0:T(128)S(1)}, s32[16]{0:T(128)}, u32[]{:S(2)}) copy-start(s32[16]{0:T(128)} %dims_ref.3) | copy-start | bytes 196
  8.1 49.3 %collective-permute-start.2 = (f32[2,512,512]{2,1,0:T(8,128)}, f32[2,512,512]{2,1,0:T(8,128)}, u32[]{:S(2)}, u32[]{:S(2)}) collective-permute-start(f32[2,512,512]{2,1,0:T(8,128)} %pick.1), channel_id=1, source_target_pairs={{0,64},{64,0},{1,65},{65,1},{2,66},{66,2},{3,67},{67,3},{4,68},{68... | collective-permute-start | bytes 6291464 | tf_op jit(solution)/shard_map/ppermute | solution.py:50
  12.9 16.3 %all-to-all-start.1 = ((f32[4,2,2,8,512]{4,3,2,1,0:T(8,128)}), f32[4,2,2,8,512]{4,3,2,1,0:T(8,128)S(1)}, u32[]{:S(2)}, u32[]{:S(2)}) async-start(f32[4,2,2,8,512]{4,3,2,1,0:T(8,128)} %get-tuple-element.20), calls=%async_computation.1 | async-start | bytes 524288 | tf_op jit(solution)/shard_map/all_to_all | solution.py:213
  19.1 3.1 %collective-permute-start.1 = (f32[2,2,8,512]{3,2,1,0:T(8,128)S(1)}, f32[2,2,8,512]{3,2,1,0:T(8,128)S(1)}, u32[]{:S(2)}, u32[]{:S(2)}) collective-permute-start(f32[2,2,8,512]{3,2,1,0:T(8,128)S(1)} %get-tuple-element.21), channel_id=1, source_target_pairs={{0,1},{1,0},{2,3},{3,2},{4,5},{5,4},{6,7},{7,6},{8,9},{9,8},{10,11... | collective-permute-start | bytes 196616 | tf_op jit(solution)/shard_map/ppermute | solution.py:215
  63.6 18.2 %all-to-all-start.2 = ((f32[8,8,8,512]{3,2,1,0:T(8,128)}), f32[8,8,8,512]{3,2,1,0:T(8,128)S(1)}, u32[]{:S(2)}, u32[]{:S(2)}) async-start(f32[8,8,8,512]{3,2,1,0:T(8,128)} %bitcast.12), calls=%async_computation.2 | async-start | bytes 2097152 | tf_op jit(solution)/shard_map/all_to_all | solution.py:259
  69.4 12.3 %collective-permute-start.3 = (f32[2,2,2,8,512]{4,3,2,1,0:T(8,128)S(1)}, f32[2,2,2,8,512]{4,3,2,1,0:T(8,128)S(1)}, u32[]{:S(2)}, u32[]{:S(2)}) collective-permute-start(f32[2,2,2,8,512]{4,3,2,1,0:T(8,128)S(1)} %pad_maximum_fusion.chip_ref), channel_id=1, source_target_pairs={{0,2},{2,0},{4,6},{6,4},{1,3},{3,1},{5,7},{7,5},{8,10},{10,8},{12,... | collective-permute-start | bytes 393224 | tf_op jit(solution)/shard_map/ppermute | solution.py:257
  81.7 5.8 %copy-start.3 = (s32[16]{0:T(128)S(1)}, s32[16]{0:T(128)}, u32[]{:S(2)}) copy-start(s32[16]{0:T(128)} %pair_ref.3) | copy-start | bytes 196
  81.8 17.2 %all-to-all-start.3 = ((f32[8,8,8,512]{3,2,1,0:T(8,128)}), f32[8,8,8,512]{3,2,1,0:T(8,128)S(1)}, u32[]{:S(2)}, u32[]{:S(2)}) async-start(f32[8,8,8,512]{3,2,1,0:T(8,128)} %bitcast.11), calls=%async_computation.3 | async-start | bytes 2097152 | tf_op jit(solution)/shard_map/all_to_all | solution.py:261
  88.0 12.5 %collective-permute-start.4 = (f32[2,2,8,512]{3,2,1,0:T(8,128)S(1)}, f32[2,2,8,512]{3,2,1,0:T(8,128)S(1)}, u32[]{:S(2)}, u32[]{:S(2)}) collective-permute-start(f32[2,2,8,512]{3,2,1,0:T(8,128)S(1)} %choose.1), channel_id=1, source_target_pairs={{0,4},{4,0},{2,6},{6,2},{1,5},{5,1},{3,7},{7,3},{8,12},{12,8},{10,... | collective-permute-start | bytes 196616 | tf_op jit(solution)/shard_map/ppermute | solution.py:278
  100.5 16.9 %all-to-all-start.4 = ((f32[8,2,8,512]{3,2,1,0:T(8,128)}), f32[8,2,8,512]{3,2,1,0:T(8,128)S(1)}, u32[]{:S(2)}, u32[]{:S(2)}) async-start(f32[8,2,8,512]{3,2,1,0:T(8,128)} %near_sum.1), calls=%async_computation.4 | async-start | bytes 524288 | tf_op jit(solution)/shard_map/all_to_all | solution.py:280
  106.7 1.6 %copy-start = (f32[2,512,512]{2,1,0:T(8,128)S(1)}, f32[2,512,512]{2,1,0:T(8,128)}, u32[]{:S(2)}) copy-start(f32[2,512,512]{2,1,0:T(8,128)} %shift_ref.1) | copy-start | bytes 6291460

commit v4 on v3

--- a/solution.py
+++ b/solution.py
@@ -7,12 +7,10 @@
 from jax.experimental.pallas import tpu as pltpu
 from jax.sharding import Mesh, PartitionSpec as P
 
-AXES = ("x", "zl", "yh", "yl", "zh", "c")
-SIZES = (4, 2, 4, 2, 4, 2)
-OPS = ("x", "zl", "yh", "yl")
+AXES = ("xh", "xl", "zl", "yh", "yl", "zh", "c")
+SIZES = (2, 2, 2, 4, 2, 4, 2)
+OPS = ("xh", "xl", "zl", "yh", "yl")
 WF = ("zh", "c")
-FAR = ("zl", "yh")
-NEAR = ("x", "yl")
 F32 = jnp.float32
 BF16 = jnp.bfloat16
 VMEM = pl.BlockSpec(memory_space=pltpu.VMEM)
@@ -91,53 +89,63 @@
 
 
 def product_kernel(
-    vector, spot_ref, g_ref, l_ref, r_ref, pair_ref, out_ref,
+    place_ref, g_ref, l_ref, r_ref, pair_ref, out_ref,
     g, ops, out, ph, pw, mh, ml, rh, rl, sems, out_sems,
 ):
     width = g.shape[-1]
     half = width // 2
-    sources = (l_ref.at[0, spot_ref[0]], pair_ref.at[0], r_ref.at[0, spot_ref[0]], pair_ref.at[1])
-    loads = [pltpu.make_async_copy(g_ref.at[:, :, :, :, vector], g, sems.at[4])] + [
+    mine = place_ref[0] // 8 % 2
+    sources = (l_ref.at[0, mine], pair_ref.at[0], r_ref.at[0, mine], pair_ref.at[1])
+    loads = [pltpu.make_async_copy(g_ref, g, sems.at[4])] + [
         pltpu.make_async_copy(source, ops.at[at], sems.at[at]) for at, source in enumerate(sources)
     ]
     for load in loads:
         load.start()
     loads[0].wait()
-    for x in range(4):
-        for z in range(2):
-            part = g[x, :, :, (z + spot_ref[0]) % 2].transpose(1, 0, 2, 3).reshape(64, width)
-            rows = pl.ds(x * 128 + z * 64, 64)
-            ph[rows], pw[rows] = halves(part)
+    for v in range(2):
+        for x in range(4):
+            for z in range(2):
+                part = g[x, :, :, (z + mine) % 2, v].transpose(1, 0, 2, 3).reshape(64, width)
+                rows = pl.ds(x * 128 + z * 64, 64)
+                ph[v, rows], pw[v, rows] = halves(part)
     for t in range(2):
         loads[1 + t].wait()
         for i in range(2):
             rows = pl.ds(i * half, half)
             high, low = halves(ops[t, rows])
-            m = times(high, ph[...]) + times(low, ph[...]) + times(high, pw[...])
-            mh[t, rows], ml[t, rows] = halves(m)
+            for v in range(2):
+                m = times(high, ph[v]) + times(low, ph[v]) + times(high, pw[v])
+                mh[v, t, rows], ml[v, t, rows] = halves(m)
     for t in range(2):
         loads[3 + t].wait()
         rh[t], rl[t] = halves(ops[2 + t])
     stores = []
-    for i in range(2):
-        rows = pl.ds(i * half, half)
-        s = times_t(mh[0, rows], rh[0]) + times_t(ml[0, rows], rh[0]) + times_t(mh[0, rows], rl[0])
-        s += times_t(mh[1, rows], rh[1]) + times_t(ml[1, rows], rh[1]) + times_t(mh[1, rows], rl[1])
-        s = s.reshape(2, 2, 4, 2, 8, width).transpose(0, 3, 1, 2, 4, 5)
-        out[pl.ds(i * 2, 2)] = s
-        place = pl.ds(i * 2, 2)
-        stores.append(pltpu.make_async_copy(out.at[place], out_ref.at[place], out_sems.at[i]))
-        stores[-1].start()
+    for v in range(2):
+        for i in range(2):
+            rows = pl.ds(i * half, half)
+            s = jnp.zeros((half, width), F32)
+            for t in range(2):
+                s += times_t(mh[v, t, rows], rh[t]) + times_t(ml[v, t, rows], rh[t])
+                s += times_t(mh[v, t, rows], rl[t])
+            s = s.reshape(2, 2, 4, 2, 8, width)
+            for xl in range(2):
+                for yl in range(2):
+                    out[i, xl, yl, :, :, v] = s[xl, :, :, yl]
+            stores.append(
+                pltpu.make_async_copy(
+                    out.at[i, :, :, :, :, v], out_ref.at[i, :, :, :, :, v], out_sems.at[v * 2 + i]
+                )
+            )
+            stores[-1].start()
     for store in stores:
         store.wait()
 
 
-def sum_kernel(one_ref, two_ref, out_ref):
-    for vector, ref in enumerate((one_ref, two_ref)):
-        total = ref[0]
-        for source in range(1, ref.shape[0]):
-            total = total + ref[source]
-        out_ref[:, vector] = total
+def sum_kernel(in_ref, out_ref):
+    total = in_ref[0]
+    for source in range(1, in_ref.shape[0]):
+        total = total + in_ref[source]
+    out_ref[...] = total
 
 
 def held_rows(place_ref, pair, chip_ref, next_ref):
@@ -218,55 +226,52 @@
     near_in = lax.cond(
         lax.optimization_barrier(jnp.bool_(True)),
         lambda value: lax.all_to_all(
-            jnp.broadcast_to(value[None], (8,) + value.shape), NEAR, 0, 0, tiled=True
+            jnp.broadcast_to(value[None], (8,) + value.shape), ("xh", "xl", "yl"), 0, 0, tiled=True
         ),
         lambda value: jnp.zeros((8,) + value.shape, F32),
         far_in,
     )
     near_in, pair_in = lax.optimization_barrier((near_in, pair_in))
 
-    products = []
-    for vector in range(2):
-        sums = pl.pallas_call(
-            functools.partial(product_kernel, vector),
-            out_shape=shape(4, 2, 2, 4, rows, width),
-            in_specs=[SMEM, HBM, HBM, HBM, HBM],
-            out_specs=HBM,
-            scratch_shapes=[
-                pltpu.VMEM((4, 2, 4, 2, rows, width), F32),
-                pltpu.VMEM((4, width, width), F32),
-                pltpu.VMEM((4, 2, 2, 4, rows, width), F32),
-                pltpu.VMEM((width, width), BF16),
-                pltpu.VMEM((width, width), BF16),
-                pltpu.VMEM((2, width, width), BF16),
-                pltpu.VMEM((2, width, width), BF16),
-                pltpu.VMEM((2, width, width), BF16),
-                pltpu.VMEM((2, width, width), BF16),
-                pltpu.SemaphoreType.DMA((5,)),
-                pltpu.SemaphoreType.DMA((2,)),
-            ],
-            compiler_params=WIDE,
-            cost_estimate=pl.CostEstimate(
-                flops=12 * 2 * 512**3, bytes_accessed=8 * 2**20, transcendentals=0
-            ),
-            name="products",
-        )(spot, near_in.reshape(4, 2, 4, 2, 2, rows, width), left_ops, right_ops, pair_in)
-        products.append(sums.reshape(8, 8, rows, width))
+    products = pl.pallas_call(
+        product_kernel,
+        out_shape=shape(2, 2, 2, 2, 4, 2, rows, width),
+        in_specs=[SMEM, HBM, HBM, HBM, HBM],
+        out_specs=HBM,
+        scratch_shapes=[
+            pltpu.VMEM((4, 2, 4, 2, 2, rows, width), F32),
+            pltpu.VMEM((4, width, width), F32),
+            pltpu.VMEM((2, 2, 2, 2, 4, 2, rows, width), F32),
+            pltpu.VMEM((2, width, width), BF16),
+            pltpu.VMEM((2, width, width), BF16),
+            pltpu.VMEM((2, 2, width, width), BF16),
+            pltpu.VMEM((2, 2, width, width), BF16),
+            pltpu.VMEM((2, width, width), BF16),
+            pltpu.VMEM((2, width, width), BF16),
+            pltpu.SemaphoreType.DMA((5,)),
+            pltpu.SemaphoreType.DMA((4,)),
+        ],
+        compiler_params=WIDE,
+        cost_estimate=pl.CostEstimate(
+            flops=24 * 2 * 512**3, bytes_accessed=8 * 2**20, transcendentals=0
+        ),
+        name="products",
+    )(place, near_in.reshape(4, 2, 4, 2, 2, rows, width), left_ops, right_ops, pair_in)
 
     chip = after(jnp.stack([live, other_core]), near_in)
     next_chip = lax.ppermute(chip, "zh", [(0, 1), (1, 0), (2, 3), (3, 2)])
 
-    near_back_one = lax.all_to_all(products[0], NEAR, 0, 0, tiled=True)
-    products[1], next_chip = lax.optimization_barrier((products[1], next_chip))
-    near_backs = [near_back_one, lax.all_to_all(products[1], NEAR, 0, 0, tiled=True)]
+    near_back = lax.all_to_all(
+        products.reshape(8, 8, 2, rows, width), ("xh", "xl", "yl"), 0, 0, tiled=True
+    )
     near_sum = pl.pallas_call(
         sum_kernel,
         out_shape=shape(8, 2, rows, width),
-        in_specs=[VMEM, VMEM],
+        in_specs=[VMEM],
         out_specs=VMEM,
         compiler_params=PARAMS,
         name="near_sum",
-    )(*near_backs)
+    )(near_back)
     chosen = pl.pallas_call(
         choose_kernel,
         out_shape=shape(blocks, 2, rows, width),
@@ -277,7 +282,7 @@
     )(place, partner, chip, next_chip)
     from_far = lax.ppermute(chosen, "zh", [(0, 2), (2, 0), (1, 3), (3, 1)])
     near_sum, from_far = lax.optimization_barrier((near_sum, from_far))
-    far_back = lax.all_to_all(near_sum, FAR, 0, 0, tiled=True)
+    far_back = lax.all_to_all(near_sum, ("zl", "yh"), 0, 0, tiled=True)
 
     shifted = pl.pallas_call(
         shift_kernel,

time: 119 us -> 117 us (0.983)
  the two profiles are of different devices: /device:TPU:10 before, /device:TPU:128 now
where the time goes in v4:
time: 117 us
  starting transfers between devices  37.9 us (32%)
  waiting for transfers between devices  29.3 us (25%)
  blocking collectives  28 us (24%)
  Pallas kernels  17.9 us (15%)
  local copies, waits for them, and re-layouts  2.62 us (2%)
    all_to_all x1, blocking collectives, per_device(): lax.all_to_all(jnp.broadcast_to(value[None], (8,) + value.shape), ('xh',...  28 us
    pallas_call x1, Pallas kernels, per_device(): pl.pallas_call(product_kernel, out_shape=shape(2, 2, 2, 2, 4, 2, rows, wi...  10.2 us
    all_to_all x1, waiting for transfers between devices, per_device(): lax.all_to_all(products.reshape(8, 8, 2, rows, width), ('xh', 'xl', 'yl')...  9.08 us
    ppermute x1, starting transfers between devices, per_device(): from_far = lax.ppermute(chosen, 'zh', [(0, 2), (2, 0), (1, 3), (3, 1)])  8.22 us
    ppermute x2, starting transfers between devices, swap(): return lax.ppermute(value, 'zl', [(0, 1), (1, 0)])  7.59 us
    all_to_all x1, starting transfers between devices, per_device(): far_in = lax.all_to_all(far_out, 'yh', 0, 0, tiled=True)  7.09 us
    all_to_all x1, waiting for transfers between devices, per_device(): far_back = lax.all_to_all(near_sum, ('zl', 'yh'), 0, 0, tiled=True)  6.51 us
    all_to_all x1, waiting for transfers between devices, per_device(): far_in = lax.all_to_all(far_out, 'yh', 0, 0, tiled=True)  6.5 us
  transfers between devices with their start and end apart: 8, of which 5 were waited for; matrix products, arithmetic and copies ran while one was open for 0% of the time, Pallas kernels for 6%

profile of v4, /device:TPU:128, one launch (start us, length us, event | category | flops | bytes accessed | tf_op | source)
XLA Modules:
  0.0 116.5 jit_solution(5098561173255184759)
XLA Ops:
  0.6 0.7 constant_dynamic-slice_fusion
  1.4 4.3 %collective-permute-start = (f32[2,8,512]{2,1,0:T(8,128)S(1)}, f32[2,8,512]{2,1,0:T(8,128)S(1)}, u32[]{:S(2)}, u32[]{:S(2)}) collective-permute-start(f32[2,8,512]{2,1,0:T(8,128)S(1)} %pad_maximum_fusion.1), channel_id=1, source_target_pairs={{0,64},{64,0},{1,65},{65,1},{2,66},{66,2},{3,67},{67,3},{4,68},{68... | collective-permute-start | bytes 98312 | tf_op jit(solution)/shard_map/ppermute | solution.py:48
  5.7 0.0 copy-start.1
  5.7 0.0 copy-start.2
  5.7 0.0 copy-start.6
  5.7 2.4 %pick.1 = f32[2,512,512]{2,1,0:T(8,128)} custom-call(s32[1]{0:T(128)} %bitcast.2.spot_ref, f32[1,2,512,512]{3,2,1,0:T(8,128)} %l_ref.1, f32[1,2,512,512]{3,2,1,0:T(8,128)} %r_ref.1), custom_call_target="tpu_custom_call" | custom-call | tf_op jit(solution)/shard_map/pick/pallas_call | solution.py:197
  8.1 3.3 %collective-permute-start.2 = (f32[2,512,512]{2,1,0:T(8,128)}, f32[2,512,512]{2,1,0:T(8,128)}, u32[]{:S(2)}, u32[]{:S(2)}) collective-permute-start(f32[2,512,512]{2,1,0:T(8,128)} %pick.1), channel_id=1, source_target_pairs={{0,64},{64,0},{1,65},{65,1},{2,66},{66,2},{3,67},{67,3},{4,68},{68... | collective-permute-start | bytes 6291464 | tf_op jit(solution)/shard_map/ppermute | solution.py:48
  11.5 0.1 pad_add_fusion.place_ref
  11.6 1.3 %spread.1 = (f32[4,2,2,8,512]{4,3,2,1,0:T(8,128)}, f32[2,2,8,512]{3,2,1,0:T(8,128)S(1)}) custom-call(s32[2]{0:T(128)S(1)} %pad_add_fusion.place_ref, s32[16]{0:T(128)S(1)} %copy-done.6, f32[2,8,512]{2,1,0:T(8,128)S(1)} %copy-done.1, f32[2,8,512]{2,1,0:T(8,128)S(1)} %copy-done.2, f32[2,8,512]{2,1,0:T(8,128)S(1)} %collective-permute-done.got_ref), custom_call_target="tpu_custom_call" | custom-call | tf_op jit(solution)/shard_map/spread/pallas_call | solution.py:213
  12.9 7.1 %all-to-all-start.1 = ((f32[4,2,2,8,512]{4,3,2,1,0:T(8,128)}), f32[4,2,2,8,512]{4,3,2,1,0:T(8,128)S(1)}, u32[]{:S(2)}, u32[]{:S(2)}) async-start(f32[4,2,2,8,512]{4,3,2,1,0:T(8,128)} %get-tuple-element.18), calls=%async_computation.1 | async-start | bytes 524288 | tf_op jit(solution)/shard_map/all_to_all | solution.py:221
  20.0 1.9 %collective-permute-start.1 = (f32[2,2,8,512]{3,2,1,0:T(8,128)S(1)}, f32[2,2,8,512]{3,2,1,0:T(8,128)S(1)}, u32[]{:S(2)}, u32[]{:S(2)}) collective-permute-start(f32[2,2,8,512]{3,2,1,0:T(8,128)S(1)} %get-tuple-element.19), channel_id=1, source_target_pairs={{0,1},{1,0},{2,3},{3,2},{4,5},{5,4},{6,7},{7,6},{8,9},{9,8},{10,11... | collective-permute-start | bytes 196616 | tf_op jit(solution)/shard_map/ppermute | solution.py:223
  21.9 1.2 %collective-permute-done.1 = f32[2,2,8,512]{3,2,1,0:T(8,128)S(1)} collective-permute-done((f32[2,2,8,512]{3,2,1,0:T(8,128)S(1)}, f32[2,2,8,512]{3,2,1,0:T(8,128)S(1)}, u32[]{:S(2)}, u32[]{:S(2)}) %collective-permute-start.1) | collective-permute-done | bytes 65568 | tf_op jit(solution)/shard_map/ppermute | solution.py:223
  23.1 6.5 %all-to-all-done.1 = f32[4,2,2,8,512]{4,3,2,1,0:T(8,128)S(1)} async-done(((f32[4,2,2,8,512]{4,3,2,1,0:T(8,128)}), f32[4,2,2,8,512]{4,3,2,1,0:T(8,128)S(1)}, u32[]{:S(2)}, u32[]{:S(2)}) %all-to-all-start.1) | async-done | bytes 262176 | tf_op jit(solution)/shard_map/all_to_all | solution.py:221
  29.6 28.2 %conditional.1 = (f32[8,4,2,2,8,512]{5,4,3,2,1,0:T(8,128)S(1)}) conditional(s32[]{:T(128)} %convert_element_type.3, () %tuple.18, f32[4,2,2,8,512]{4,3,2,1,0:T(8,128)S(1)} %all-to-all-done.1), branch_computations={%region_0.1_spmd, %region_1.2_spmd} | conditional | bytes 6553608 | solution.py:226
  29.6 0.3 broadcast_in_dim.0
  29.9 28.0 %all_to_all.19 = f32[8,4,2,2,8,512]{5,4,3,2,1,0:T(8,128)S(1)} all-to-all(f32[8,4,2,2,8,512]{5,4,3,2,1,0:T(8,128)S(1)} %broadcast_in_dim.0), channel_id=1, replica_groups=mesh['xh'=2,'xl'=2,'zl'=2,'yh'=4,'yl'=2,'zh'=4,'c'=2] {'xh','xl','yl'}, dimensions={0} | all-to-all | bytes 4194304 | tf_op jit(solution)/shard_map/cond/branch_1_fun/all_to_all | solution.py:228
  57.8 0.0 collective-permute-done.2.pair_ref
  57.8 10.2 %products.1 = f32[2,2,2,2,4,2,8,512]{7,6,5,4,3,2,1,0:T(8,128)} custom-call(s32[2]{0:T(128)} %copy-done.3, f32[4,2,4,2,2,8,512]{6,5,4,3,2,1,0:T(8,128)S(1)} %bitcast.8, f32[1,2,512,512]{3,2,1,0:T(8,128)} %l_ref.1, f32[1,2,512,512]{3,2,1,0:T(8,128)} %r_ref.1, f32[2,512,512]{2,1,0:T(8,128)} %collective-permute-done.2.pair_ref), custom_call_target="tpu_custom_call" | custom-call | flops 6442450944 | bytes 8388608 | tf_op jit(solution)/shard_map/products/pallas_call | solution.py:236
  68.0 0.0 copy-start.4
  68.0 0.0 copy-start.5
  68.0 4.9 %all-to-all-start.2 = ((f32[8,8,2,8,512]{4,3,2,1,0:T(8,128)}), f32[8,8,2,8,512]{4,3,2,1,0:T(8,128)S(1)}, u32[]{:S(2)}, u32[]{:S(2)}) async-start(f32[8,8,2,8,512]{4,3,2,1,0:T(8,128)} %bitcast.9), calls=%async_computation.2 | async-start | bytes 4194304 | tf_op jit(solution)/shard_map/all_to_all | solution.py:264
  73.0 1.9 %collective-permute-start.3 = (f32[2,2,2,8,512]{4,3,2,1,0:T(8,128)S(1)}, f32[2,2,2,8,512]{4,3,2,1,0:T(8,128)S(1)}, u32[]{:S(2)}, u32[]{:S(2)}) collective-permute-start(f32[2,2,2,8,512]{4,3,2,1,0:T(8,128)S(1)} %pad_maximum_fusion.chip_ref), channel_id=1, source_target_pairs={{0,2},{2,0},{4,6},{6,4},{1,3},{3,1},{5,7},{7,5},{8,10},{10,8},{12,... | collective-permute-start | bytes 393224 | tf_op jit(solution)/shard_map/ppermute | solution.py:262
  74.9 5.9 %collective-permute-done.3.next_ref = f32[2,2,2,8,512]{4,3,2,1,0:T(8,128)S(1)} collective-permute-done((f32[2,2,2,8,512]{4,3,2,1,0:T(8,128)S(1)}, f32[2,2,2,8,512]{4,3,2,1,0:T(8,128)S(1)}, u32[]{:S(2)}, u32[]{:S(2)}) %collective-permute-start.3) | collective-permute-done | bytes 131104 | tf_op jit(solution)/shard_map/ppermute | solution.py:262
  80.8 0.6 choose.1
  81.4 8.2 %collective-permute-start.4 = (f32[2,2,8,512]{3,2,1,0:T(8,128)S(1)}, f32[2,2,8,512]{3,2,1,0:T(8,128)S(1)}, u32[]{:S(2)}, u32[]{:S(2)}) collective-permute-start(f32[2,2,8,512]{3,2,1,0:T(8,128)S(1)} %choose.1), channel_id=1, source_target_pairs={{0,4},{4,0},{2,6},{6,2},{1,5},{5,1},{3,7},{7,3},{8,12},{12,8},{10,... | collective-permute-start | bytes 196616 | tf_op jit(solution)/shard_map/ppermute | solution.py:283
  89.6 9.1 %all-to-all-done.2.in_ref = f32[8,8,2,8,512]{4,3,2,1,0:T(8,128)S(1)} async-done(((f32[8,8,2,8,512]{4,3,2,1,0:T(8,128)}), f32[8,8,2,8,512]{4,3,2,1,0:T(8,128)S(1)}, u32[]{:S(2)}, u32[]{:S(2)}) %all-to-all-start.2) | async-done | bytes 2097184 | tf_op jit(solution)/shard_map/all_to_all | solution.py:264
  98.7 0.8 near_sum.1
  99.5 6.2 %all-to-all-start.3 = ((f32[8,2,8,512]{3,2,1,0:T(8,128)}), f32[8,2,8,512]{3,2,1,0:T(8,128)S(1)}, u32[]{:S(2)}, u32[]{:S(2)}) async-start(f32[8,2,8,512]{3,2,1,0:T(8,128)} %near_sum.1), calls=%async_computation.3 | async-start | bytes 524288 | tf_op jit(solution)/shard_map/all_to_all | solution.py:285
  105.7 1.6 %copy-done = f32[2,512,512]{2,1,0:T(8,128)S(1)} copy-done((f32[2,512,512]{2,1,0:T(8,128)S(1)}, f32[2,512,512]{2,1,0:T(8,128)}, u32[]{:S(2)}) %copy-start) | copy-done | bytes 2097176
  107.3 1.5 %shift.1.shifted_ref = f32[2,2,8,512]{3,2,1,0:T(8,128)S(1)} custom-call(s32[2]{0:T(128)S(1)} %copy-done.4, s32[16]{0:T(128)S(1)} %copy-done.5, f32[2,2,2,8,512]{4,3,2,1,0:T(8,128)S(1)} %pad_maximum_fusion.chip_ref, f32[2,2,2,8,512]{4,3,2,1,0:T(8,128)S(1)} %collective-permute-done.3.next_ref, f32[2,2,8,512]{3,2,1,0:T(8,128)S(1)} %collective-permute-done.4.far_ref, ...), custom_call_target="tpu_custom_call" | custom-call | flops 50331648 | bytes 3145728 | tf_op jit(solution)/shard_map/shift/pallas_call | solution.py:287
  108.8 6.5 %all-to-all-done.3.back_ref = f32[8,2,8,512]{3,2,1,0:T(8,128)S(1)} async-done(((f32[8,2,8,512]{3,2,1,0:T(8,128)}), f32[8,2,8,512]{3,2,1,0:T(8,128)S(1)}, u32[]{:S(2)}, u32[]{:S(2)}) %all-to-all-start.3) | async-done | bytes 262176 | tf_op jit(solution)/shard_map/all_to_all | solution.py:285
  115.3 1.2 %finish.1 = (f32[2,8,512]{2,1,0:T(8,128)}, f32[2,8,512]{2,1,0:T(8,128)}) custom-call(s32[2]{0:T(128)S(1)} %copy-done.4, s32[16]{0:T(128)S(1)} %copy-done.6, f32[8,2,8,512]{3,2,1,0:T(8,128)S(1)} %all-to-all-done.3.back_ref, f32[2,2,8,512]{3,2,1,0:T(8,128)S(1)} %shift.1.shifted_ref), custom_call_target="tpu_custom_call" | custom-call | tf_op jit(solution)/shard_map/finish/pallas_call | solution.py:299
  (12 shorter events, 0.0 us)
Async XLA Ops:
  1.4 6.7 %collective-permute-start = (f32[2,8,512]{2,1,0:T(8,128)S(1)}, f32[2,8,512]{2,1,0:T(8,128)S(1)}, u32[]{:S(2)}, u32[]{:S(2)}) collective-permute-start(f32[2,8,512]{2,1,0:T(8,128)S(1)} %pad_maximum_fusion.1), channel_id=1, source_target_pairs={{0,64},{64,0},{1,65},{65,1},{2,66},{66,2},{3,67},{67,3},{4,68},{68... | collective-permute-start | bytes 98312 | tf_op jit(solution)/shard_map/ppermute | solution.py:48
  5.7 5.9 %copy-start.1 = (f32[2,8,512]{2,1,0:T(8,128)S(1)}, f32[2,8,512]{2,1,0:T(8,128)}, u32[]{:S(2)}) copy-start(f32[2,8,512]{2,1,0:T(8,128)} %one_ref.1) | copy-start | bytes 98308
  5.7 5.9 %copy-start.2 = (f32[2,8,512]{2,1,0:T(8,128)S(1)}, f32[2,8,512]{2,1,0:T(8,128)}, u32[]{:S(2)}) copy-start(f32[2,8,512]{2,1,0:T(8,128)} %two_ref.1) | copy-start | bytes 98308
  5.7 5.9 %copy-start.6 = (s32[16]{0:T(128)S(1)}, s32[16]{0:T(128)}, u32[]{:S(2)}) copy-start(s32[16]{0:T(128)} %dims_ref.3) | copy-start | bytes 196
  8.1 49.7 %collective-permute-start.2 = (f32[2,512,512]{2,1,0:T(8,128)}, f32[2,512,512]{2,1,0:T(8,128)}, u32[]{:S(2)}, u32[]{:S(2)}) collective-permute-start(f32[2,512,512]{2,1,0:T(8,128)} %pick.1), channel_id=1, source_target_pairs={{0,64},{64,0},{1,65},{65,1},{2,66},{66,2},{3,67},{67,3},{4,68},{68... | collective-permute-start | bytes 6291464 | tf_op jit(solution)/shard_map/ppermute | solution.py:48
  11.6 18.1 %copy-start.3 = (s32[2]{0:T(128)}, s32[2]{0:T(128)S(1)}, u32[]{:S(2)}) copy-start(s32[2]{0:T(128)S(1)} %pad_add_fusion.place_ref) | copy-start | bytes 28
  12.9 16.7 %all-to-all-start.1 = ((f32[4,2,2,8,512]{4,3,2,1,0:T(8,128)}), f32[4,2,2,8,512]{4,3,2,1,0:T(8,128)S(1)}, u32[]{:S(2)}, u32[]{:S(2)}) async-start(f32[4,2,2,8,512]{4,3,2,1,0:T(8,128)} %get-tuple-element.18), calls=%async_computation.1 | async-start | bytes 524288 | tf_op jit(solution)/shard_map/all_to_all | solution.py:221
  20.0 3.1 %collective-permute-start.1 = (f32[2,2,8,512]{3,2,1,0:T(8,128)S(1)}, f32[2,2,8,512]{3,2,1,0:T(8,128)S(1)}, u32[]{:S(2)}, u32[]{:S(2)}) collective-permute-start(f32[2,2,8,512]{3,2,1,0:T(8,128)S(1)} %get-tuple-element.19), channel_id=1, source_target_pairs={{0,1},{1,0},{2,3},{3,2},{4,5},{5,4},{6,7},{7,6},{8,9},{9,8},{10,11... | collective-permute-start | bytes 196616 | tf_op jit(solution)/shard_map/ppermute | solution.py:223
  68.0 12.8 %copy-start.4 = (s32[2]{0:T(128)S(1)}, s32[2]{0:T(128)}, u32[]{:S(2)}) copy-start(s32[2]{0:T(128)} %copy-done.3) | copy-start | bytes 28
  68.0 12.8 %copy-start.5 = (s32[16]{0:T(128)S(1)}, s32[16]{0:T(128)}, u32[]{:S(2)}) copy-start(s32[16]{0:T(128)} %pair_ref.3) | copy-start | bytes 196
  68.0 30.7 %all-to-all-start.2 = ((f32[8,8,2,8,512]{4,3,2,1,0:T(8,128)}), f32[8,8,2,8,512]{4,3,2,1,0:T(8,128)S(1)}, u32[]{:S(2)}, u32[]{:S(2)}) async-start(f32[8,8,2,8,512]{4,3,2,1,0:T(8,128)} %bitcast.9), calls=%async_computation.2 | async-start | bytes 4194304 | tf_op jit(solution)/shard_map/all_to_all | solution.py:264
  73.0 7.9 %collective-permute-start.3 = (f32[2,2,2,8,512]{4,3,2,1,0:T(8,128)S(1)}, f32[2,2,2,8,512]{4,3,2,1,0:T(8,128)S(1)}, u32[]{:S(2)}, u32[]{:S(2)}) collective-permute-start(f32[2,2,2,8,512]{4,3,2,1,0:T(8,128)S(1)} %pad_maximum_fusion.chip_ref), channel_id=1, source_target_pairs={{0,2},{2,0},{4,6},{6,4},{1,3},{3,1},{5,7},{7,5},{8,10},{10,8},{12,... | collective-permute-start | bytes 393224 | tf_op jit(solution)/shard_map/ppermute | solution.py:262
  81.4 18.1 %collective-permute-start.4 = (f32[2,2,8,512]{3,2,1,0:T(8,128)S(1)}, f32[2,2,8,512]{3,2,1,0:T(8,128)S(1)}, u32[]{:S(2)}, u32[]{:S(2)}) collective-permute-start(f32[2,2,8,512]{3,2,1,0:T(8,128)S(1)} %choose.1), channel_id=1, source_target_pairs={{0,4},{4,0},{2,6},{6,2},{1,5},{5,1},{3,7},{7,3},{8,12},{12,8},{10,... | collective-permute-start | bytes 196616 | tf_op jit(solution)/shard_map/ppermute | solution.py:283
  99.5 15.8 %all-to-all-start.3 = ((f32[8,2,8,512]{3,2,1,0:T(8,128)}), f32[8,2,8,512]{3,2,1,0:T(8,128)S(1)}, u32[]{:S(2)}, u32[]{:S(2)}) async-start(f32[8,2,8,512]{3,2,1,0:T(8,128)} %near_sum.1), calls=%async_computation.3 | async-start | bytes 524288 | tf_op jit(solution)/shard_map/all_to_all | solution.py:285
  105.7 1.6 %copy-start = (f32[2,512,512]{2,1,0:T(8,128)S(1)}, f32[2,512,512]{2,1,0:T(8,128)}, u32[]{:S(2)}) copy-start(f32[2,512,512]{2,1,0:T(8,128)} %shift_ref.1) | copy-start | bytes 6291460

commit v5 on v4

--- a/solution.py
+++ b/solution.py
@@ -2,6 +2,7 @@
 
 import jax
 import jax.numpy as jnp
+import numpy as np
 from jax import lax
 from jax.experimental import pallas as pl
 from jax.experimental.pallas import tpu as pltpu
@@ -17,7 +18,18 @@
 SMEM = pl.BlockSpec(memory_space=pltpu.SMEM)
 HBM = pl.BlockSpec(memory_space=pl.ANY)
 PARAMS = pltpu.CompilerParams(vmem_limit_bytes=48 * 1024 * 1024)
+OWN = pltpu.CompilerParams(vmem_limit_bytes=46 * 1024 * 1024)
+MAIN = pltpu.CompilerParams(vmem_limit_bytes=48 * 1024 * 1024)
 WIDE = pltpu.CompilerParams(vmem_limit_bytes=60 * 1024 * 1024)
+
+
+def far_groups():
+    device = np.arange(512).reshape(4, 2, 4, 2, 4, 2)
+    groups = []
+    for parity in range(2):
+        lines = np.stack([device[:, 0, :, parity], device[:, 1, :, 1 - parity]])
+        groups.extend(lines.transpose(1, 3, 4, 0, 2).reshape(-1, 8).tolist())
+    return groups
 
 
 def shape(*dims):
@@ -37,9 +49,9 @@
     return lax.dot_general(a, b, (((1,), (1,)), ((), ())), preferred_element_type=F32)
 
 
-def live_mask(place, place_ref, dims_ref, block, rows, width):
+def live_mask(place_ref, dims_ref, block, rows, width):
     size = dims_ref[place_ref[1] * 2 + block]
-    row = place * rows + lax.broadcasted_iota(jnp.int32, (rows, width), 0)
+    row = place_ref[0] * rows + lax.broadcasted_iota(jnp.int32, (rows, width), 0)
     column = lax.broadcasted_iota(jnp.int32, (rows, width), 1)
     return (row < size) & (column < size)
 
@@ -71,33 +83,24 @@
         copy.wait()
 
 
-def spread_kernel(place_ref, dims_ref, one_ref, two_ref, got_ref, far_ref, live_ref):
+def spread_kernel(place_ref, dims_ref, one_ref, two_ref, far_ref, live_ref):
     blocks, rows, width = one_ref.shape
-    mine = place_ref[0] // 8 % 2
     for block in range(blocks):
-        mask = live_mask(place_ref[0], place_ref, dims_ref, block, rows, width)
+        mask = live_mask(place_ref, dims_ref, block, rows, width)
         for vector, ref in enumerate((one_ref, two_ref)):
-            live_ref[block, vector] = jnp.where(mask, ref[block], 0.0)
-    neighbour = place_ref[0] + 8 - 16 * mine
-    mask = live_mask(neighbour, place_ref, dims_ref, mine, rows, width)
-    for vector in range(2):
-        own = live_ref[mine, vector]
-        got = jnp.where(mask, got_ref[vector], 0.0)
-        for slot in range(4):
-            far_ref[slot, 0, vector] = own
-            far_ref[slot, 1, vector] = got
-
-
-def product_kernel(
-    place_ref, g_ref, l_ref, r_ref, pair_ref, out_ref,
-    g, ops, out, ph, pw, mh, ml, rh, rl, sems, out_sems,
-):
+            live = jnp.where(mask, ref[block], 0.0)
+            live_ref[block, vector] = live
+            for slot in range(4):
+                far_ref[block * 4 + slot, vector] = live
+
+
+def own_kernel(place_ref, g_ref, l_ref, ph, pw, mh, ml, g, left, sems):
     width = g.shape[-1]
     half = width // 2
     mine = place_ref[0] // 8 % 2
-    sources = (l_ref.at[0, mine], pair_ref.at[0], r_ref.at[0, mine], pair_ref.at[1])
-    loads = [pltpu.make_async_copy(g_ref, g, sems.at[4])] + [
-        pltpu.make_async_copy(source, ops.at[at], sems.at[at]) for at, source in enumerate(sources)
+    loads = [
+        pltpu.make_async_copy(g_ref, g, sems.at[0]),
+        pltpu.make_async_copy(l_ref.at[0, mine], left, sems.at[1]),
     ]
     for load in loads:
         load.start()
@@ -105,36 +108,56 @@
     for v in range(2):
         for x in range(4):
             for z in range(2):
-                part = g[x, :, :, (z + mine) % 2, v].transpose(1, 0, 2, 3).reshape(64, width)
+                parts = [g[x, (yl + z + mine) % 2, z, :, v] for yl in range(2)]
+                part = jnp.stack(parts, axis=1).reshape(64, width)
                 rows = pl.ds(x * 128 + z * 64, 64)
                 ph[v, rows], pw[v, rows] = halves(part)
+    loads[1].wait()
+    for i in range(2):
+        rows = pl.ds(i * half, half)
+        high, low = halves(left[rows])
+        for v in range(2):
+            m = times(high, ph[v]) + times(low, ph[v]) + times(high, pw[v])
+            mh[v, rows], ml[v, rows] = halves(m)
+
+
+def product_kernel(
+    place_ref, ph, pw, own_h, own_l, r_ref, pair_ref, out_ref,
+    ops, out, mh, ml, rh, rl, sems, out_sems,
+):
+    width = ops.shape[-1]
+    half = width // 2
+    mine = place_ref[0] // 8 % 2
+    sources = (pair_ref.at[0], r_ref.at[0, mine], pair_ref.at[1])
+    loads = [
+        pltpu.make_async_copy(source, ops.at[at], sems.at[at]) for at, source in enumerate(sources)
+    ]
+    for load in loads:
+        load.start()
+    loads[0].wait()
+    for i in range(2):
+        rows = pl.ds(i * half, half)
+        high, low = halves(ops[0, rows])
+        for v in range(2):
+            m = times(high, ph[v]) + times(low, ph[v]) + times(high, pw[v])
+            mh[v, rows], ml[v, rows] = halves(m)
     for t in range(2):
         loads[1 + t].wait()
-        for i in range(2):
-            rows = pl.ds(i * half, half)
-            high, low = halves(ops[t, rows])
-            for v in range(2):
-                m = times(high, ph[v]) + times(low, ph[v]) + times(high, pw[v])
-                mh[v, t, rows], ml[v, t, rows] = halves(m)
-    for t in range(2):
-        loads[3 + t].wait()
-        rh[t], rl[t] = halves(ops[2 + t])
+        rh[t], rl[t] = halves(ops[1 + t])
     stores = []
     for v in range(2):
         for i in range(2):
             rows = pl.ds(i * half, half)
-            s = jnp.zeros((half, width), F32)
-            for t in range(2):
-                s += times_t(mh[v, t, rows], rh[t]) + times_t(ml[v, t, rows], rh[t])
-                s += times_t(mh[v, t, rows], rl[t])
+            s = times_t(own_h[v, rows], rh[0]) + times_t(own_l[v, rows], rh[0])
+            s += times_t(own_h[v, rows], rl[0]) + times_t(mh[v, rows], rh[1])
+            s += times_t(ml[v, rows], rh[1]) + times_t(mh[v, rows], rl[1])
             s = s.reshape(2, 2, 4, 2, 8, width)
             for xl in range(2):
                 for yl in range(2):
                     out[i, xl, yl, :, :, v] = s[xl, :, :, yl]
+            place = (i, slice(None), slice(None), slice(None), slice(None), v)
             stores.append(
-                pltpu.make_async_copy(
-                    out.at[i, :, :, :, :, v], out_ref.at[i, :, :, :, :, v], out_sems.at[v * 2 + i]
-                )
+                pltpu.make_async_copy(out.at[place], out_ref.at[place], out_sems.at[v * 2 + i])
             )
             stores[-1].start()
     for store in stores:
@@ -175,7 +198,7 @@
 def final_kernel(place_ref, dims_ref, back_ref, shifted_ref, one_ref, two_ref):
     blocks, rows, width = one_ref.shape
     for block in range(blocks):
-        mask = live_mask(place_ref[0], place_ref, dims_ref, block, rows, width)
+        mask = live_mask(place_ref, dims_ref, block, rows, width)
         for vector, ref in enumerate((one_ref, two_ref)):
             total = shifted_ref[block, vector]
             for source in range(4):
@@ -189,11 +212,6 @@
 
     mine = lax.axis_index("zl").astype(jnp.int32)
     spot = mine[None]
-    got = swap(
-        jnp.stack(
-            [lax.dynamic_index_in_dim(psi, 1 - mine, 0, False) for psi in (psi_one, psi_two)]
-        )
-    )
     pair_out = pl.pallas_call(
         pick_kernel,
         out_shape=shape(2, width, width),
@@ -207,18 +225,19 @@
         compiler_params=WIDE,
         name="pick",
     )(spot, left_ops, right_ops)
-    got, pair_out = lax.optimization_barrier((got, pair_out))
     pair_in = swap(pair_out)
 
     far_out, live = pl.pallas_call(
         spread_kernel,
-        out_shape=(shape(4, 2, 2, rows, width), shape(blocks, 2, rows, width)),
-        in_specs=[SMEM, SMEM, VMEM, VMEM, VMEM],
+        out_shape=(shape(8, 2, rows, width), shape(blocks, 2, rows, width)),
+        in_specs=[SMEM, SMEM, VMEM, VMEM],
         out_specs=(VMEM, VMEM),
         compiler_params=PARAMS,
         name="spread",
-    )(place, block_dims, psi_one, psi_two, got)
-    far_in = lax.all_to_all(far_out, "yh", 0, 0, tiled=True)
+    )(place, block_dims, psi_one, psi_two)
+    far_in = lax.all_to_all(
+        far_out, AXES, 0, 0, tiled=True, axis_index_groups=far_groups()
+    )
 
     other_core = lax.ppermute(live, "c", [(0, 1), (1, 0)])
     far_in, other_core = lax.optimization_barrier((far_in, other_core))
@@ -231,32 +250,46 @@
         lambda value: jnp.zeros((8,) + value.shape, F32),
         far_in,
     )
-    near_in, pair_in = lax.optimization_barrier((near_in, pair_in))
+    near_in = lax.optimization_barrier(near_in)
+    half_array = jax.ShapeDtypeStruct((2, width, width), BF16)
+    own = pl.pallas_call(
+        own_kernel,
+        out_shape=(half_array,) * 4,
+        in_specs=[SMEM, HBM, HBM],
+        out_specs=(VMEM,) * 4,
+        scratch_shapes=[
+            pltpu.VMEM((4, 2, 2, 4, 2, rows, width), F32),
+            pltpu.VMEM((width, width), F32),
+            pltpu.SemaphoreType.DMA((2,)),
+        ],
+        compiler_params=OWN,
+        cost_estimate=pl.CostEstimate(
+            flops=6 * 2 * 512**3, bytes_accessed=7 * 2**20, transcendentals=0
+        ),
+        name="own",
+    )(place, near_in.reshape(4, 2, 2, 4, 2, rows, width), left_ops)
 
     products = pl.pallas_call(
         product_kernel,
         out_shape=shape(2, 2, 2, 2, 4, 2, rows, width),
-        in_specs=[SMEM, HBM, HBM, HBM, HBM],
+        in_specs=[SMEM, VMEM, VMEM, VMEM, VMEM, HBM, HBM],
         out_specs=HBM,
         scratch_shapes=[
-            pltpu.VMEM((4, 2, 4, 2, 2, rows, width), F32),
-            pltpu.VMEM((4, width, width), F32),
+            pltpu.VMEM((3, width, width), F32),
             pltpu.VMEM((2, 2, 2, 2, 4, 2, rows, width), F32),
             pltpu.VMEM((2, width, width), BF16),
             pltpu.VMEM((2, width, width), BF16),
-            pltpu.VMEM((2, 2, width, width), BF16),
-            pltpu.VMEM((2, 2, width, width), BF16),
             pltpu.VMEM((2, width, width), BF16),
             pltpu.VMEM((2, width, width), BF16),
-            pltpu.SemaphoreType.DMA((5,)),
+            pltpu.SemaphoreType.DMA((3,)),
             pltpu.SemaphoreType.DMA((4,)),
         ],
-        compiler_params=WIDE,
+        compiler_params=MAIN,
         cost_estimate=pl.CostEstimate(
-            flops=24 * 2 * 512**3, bytes_accessed=8 * 2**20, transcendentals=0
+            flops=18 * 2 * 512**3, bytes_accessed=9 * 2**20, transcendentals=0
         ),
         name="products",
-    )(place, near_in.reshape(4, 2, 4, 2, 2, rows, width), left_ops, right_ops, pair_in)
+    )(place, *own, right_ops, pair_in)
 
     chip = after(jnp.stack([live, other_core]), near_in)
     next_chip = lax.ppermute(chip, "zh", [(0, 1), (1, 0), (2, 3), (3, 2)])

time: 117 us -> 115 us (0.983)
  starting transfers between devices: 37.9 us -> 34.3 us
  Pallas kernels: 17.9 us -> 20.2 us
    pallas_call x1 -> x2, Pallas kernels: 1.31 us -> 5.52 us  [the longest x1 4.24 us: per_device(): pl.pallas_call(own_kernel, out_shape=(half_array,) * 4, in_specs=[SMEM, H...]
    ppermute x2 -> x1, starting transfers between devices: 7.59 us -> 4.28 us  [swap(): return lax.ppermute(value, 'zl', [(0, 1), (1, 0)])]
    pallas_call x1, Pallas kernels: 10.2 us -> 8.14 us  [per_device(): pl.pallas_call(product_kernel, out_shape=shape(2, 2, 2, 2, 4, 2, rows, wi...]
    all_to_all x1, starting transfers between devices: 4.92 us -> 3.61 us  [per_device(): lax.all_to_all(products.reshape(8, 8, 2, rows, width), ('xh', 'xl', 'yl')...]
  transfers between devices with their start and end apart: 8 -> 7, of which waited for: 5 -> 5; matrix products, arithmetic and copies ran while one was open for 0% -> 0% of each run, Pallas kernels for 6% -> 7%
where the time goes in v5:
time: 115 us
  starting transfers between devices  34.3 us (30%)
  blocking collectives  29 us (25%)
  waiting for transfers between devices  28.6 us (25%)
  Pallas kernels  20.2 us (18%)
  local copies, waits for them, and re-layouts  1.87 us (2%)
    all_to_all x1, blocking collectives, per_device(): lax.all_to_all(jnp.broadcast_to(value[None], (8,) + value.shape), ('xh',...  29 us
    ppermute x1, starting transfers between devices, per_device(): from_far = lax.ppermute(chosen, 'zh', [(0, 2), (2, 0), (1, 3), (3, 1)])  8.29 us
    pallas_call x1, Pallas kernels, per_device(): pl.pallas_call(product_kernel, out_shape=shape(2, 2, 2, 2, 4, 2, rows, wi...  8.14 us
    all_to_all x1, waiting for transfers between devices, per_device(): lax.all_to_all(products.reshape(8, 8, 2, rows, width), ('xh', 'xl', 'yl')...  7.94 us
    all_to_all x1, starting transfers between devices, per_device(): far_back = lax.all_to_all(near_sum, ('zl', 'yh'), 0, 0, tiled=True)  7.14 us
    all_to_all x1, starting transfers between devices, per_device(): lax.all_to_all(far_out, AXES, 0, 0, tiled=True, axis_index_groups=far_gro...  7.1 us
    all_to_all x1, waiting for transfers between devices, per_device(): lax.all_to_all(far_out, AXES, 0, 0, tiled=True, axis_index_groups=far_gro...  7.09 us
    all_to_all x1, waiting for transfers between devices, per_device(): far_back = lax.all_to_all(near_sum, ('zl', 'yh'), 0, 0, tiled=True)  6.51 us
  transfers between devices with their start and end apart: 7, of which 5 were waited for; matrix products, arithmetic and copies ran while one was open for 0% of the time, Pallas kernels for 7%

profile of v5, /device:TPU:128, one launch (start us, length us, event | category | flops | bytes accessed | tf_op | source)
XLA Modules:
  0.0 114.7 jit_solution(12792191865830414615)
XLA Ops:
  0.6 0.0 copy-start.2
  0.7 2.4 %pick.1 = f32[2,512,512]{2,1,0:T(8,128)} custom-call(s32[1]{0:T(128)} %bitcast.3.spot_ref, f32[1,2,512,512]{3,2,1,0:T(8,128)} %left_ref.1, f32[1,2,512,512]{3,2,1,0:T(8,128)} %r_ref.1), custom_call_target="tpu_custom_call" | custom-call | tf_op jit(solution)/shard_map/pick/pallas_call | solution.py:215
  3.1 4.3 %collective-permute-start.1 = (f32[2,512,512]{2,1,0:T(8,128)}, f32[2,512,512]{2,1,0:T(8,128)}, u32[]{:S(2)}, u32[]{:S(2)}) collective-permute-start(f32[2,512,512]{2,1,0:T(8,128)} %pick.1), channel_id=1, source_target_pairs={{0,64},{64,0},{1,65},{65,1},{2,66},{66,2},{3,67},{67,3},{4,68},{68... | collective-permute-start | bytes 6291464 | tf_op jit(solution)/shard_map/ppermute | solution.py:60
  7.4 0.1 pad_add_fusion.place_ref
  7.5 0.0 copy-done.3
  7.5 1.3 %spread.1 = (f32[8,2,8,512]{3,2,1,0:T(8,128)}, f32[2,2,8,512]{3,2,1,0:T(8,128)S(1)}) custom-call(s32[2]{0:T(128)S(1)} %pad_add_fusion.place_ref, s32[16]{0:T(128)S(1)} %copy-done.5, f32[2,8,512]{2,1,0:T(8,128)S(1)} %copy-done.2, f32[2,8,512]{2,1,0:T(8,128)S(1)} %copy-done.3), custom_call_target="tpu_custom_call" | custom-call | tf_op jit(solution)/shard_map/spread/pallas_call | solution.py:230
  8.8 7.1 %all-to-all-start.1 = ((f32[8,2,8,512]{3,2,1,0:T(8,128)}), f32[8,2,8,512]{3,2,1,0:T(8,128)S(1)}, u32[]{:S(2)}, u32[]{:S(2)}) async-start(f32[8,2,8,512]{3,2,1,0:T(8,128)} %get-tuple-element.17), calls=%async_computation.1 | async-start | bytes 524288 | tf_op jit(solution)/shard_map/all_to_all | solution.py:238
  15.9 1.9 %collective-permute-start = (f32[2,2,8,512]{3,2,1,0:T(8,128)S(1)}, f32[2,2,8,512]{3,2,1,0:T(8,128)S(1)}, u32[]{:S(2)}, u32[]{:S(2)}) collective-permute-start(f32[2,2,8,512]{3,2,1,0:T(8,128)S(1)} %get-tuple-element.18), channel_id=1, source_target_pairs={{0,1},{1,0},{2,3},{3,2},{4,5},{5,4},{6,7},{7,6},{8,9},{9,8},{10,11... | collective-permute-start | bytes 196616 | tf_op jit(solution)/shard_map/ppermute | solution.py:242
  17.8 0.0 copy-start
  17.8 1.2 %collective-permute-done = f32[2,2,8,512]{3,2,1,0:T(8,128)S(1)} collective-permute-done((f32[2,2,8,512]{3,2,1,0:T(8,128)S(1)}, f32[2,2,8,512]{3,2,1,0:T(8,128)S(1)}, u32[]{:S(2)}, u32[]{:S(2)}) %collective-permute-start) | collective-permute-done | bytes 65568 | tf_op jit(solution)/shard_map/ppermute | solution.py:242
  19.0 7.1 %all-to-all-done.1 = f32[8,2,8,512]{3,2,1,0:T(8,128)S(1)} async-done(((f32[8,2,8,512]{3,2,1,0:T(8,128)}), f32[8,2,8,512]{3,2,1,0:T(8,128)S(1)}, u32[]{:S(2)}, u32[]{:S(2)}) %all-to-all-start.1) | async-done | bytes 262176 | tf_op jit(solution)/shard_map/all_to_all | solution.py:238
  26.1 29.2 %conditional.1 = (f32[8,8,2,8,512]{4,3,2,1,0:T(8,128)}) conditional(s32[]{:T(128)} %convert_element_type.3, () %tuple.16, f32[8,2,8,512]{3,2,1,0:T(8,128)S(1)} %all-to-all-done.1), branch_computations={%region_0.0_spmd, %region_1.0_spmd} | conditional | bytes 6553608 | solution.py:245
  26.1 0.3 broadcast_in_dim.0
  26.4 29.0 %all_to_all.19 = f32[8,8,2,8,512]{4,3,2,1,0:T(8,128)} all-to-all(f32[8,8,2,8,512]{4,3,2,1,0:T(8,128)S(1)} %broadcast_in_dim.0), channel_id=1, replica_groups=mesh['xh'=2,'xl'=2,'zl'=2,'yh'=4,'yl'=2,'zh'=4,'c'=2] {'xh','xl','yl'}, dimensions={0} | all-to-all | bytes 4194304 | tf_op jit(solution)/shard_map/cond/branch_1_fun/all_to_all | solution.py:247
  55.3 0.0 copy-done
  55.4 4.2 %own.1 = (bf16[2,512,512]{2,1,0:T(8,128)(2,1)S(1)}, bf16[2,512,512]{2,1,0:T(8,128)(2,1)S(1)}, bf16[2,512,512]{2,1,0:T(8,128)(2,1)S(1)}, bf16[2,512,512]{2,1,0:T(8,128)(2,1)S(1)}) custom-call(s32[2]{0:T(128)S(1)} %pad_add_fusion.place_ref, f32[4,2,2,4,2,8,512]{6,5,4,3,2,1,0:T(8,128)} %bitcast.8, f32[1,2,512,512]{3,2,1,0:T(8,128)S(1)} %copy-done), custom_call_target="tpu_custom_call" | custom-call | flops 1610612736 | bytes 7340032 | tf_op jit(solution)/shard_map/own/pallas_call | solution.py:255
  59.6 0.0 collective-permute-done.1.pair_ref
  59.6 8.1 %products.1 = f32[2,2,2,2,4,2,8,512]{7,6,5,4,3,2,1,0:T(8,128)} custom-call(s32[2]{0:T(128)S(1)} %pad_add_fusion.place_ref, bf16[2,512,512]{2,1,0:T(8,128)(2,1)S(1)} %get-tuple-element.20.ph, bf16[2,512,512]{2,1,0:T(8,128)(2,1)S(1)} %get-tuple-element.21.pw, bf16[2,512,512]{2,1,0:T(8,128)(2,1)S(1)} %get-tuple-element.22.own_h, ...), custom_call_target="tpu_custom_call" | custom-call | flops 4831838208 | bytes 9437184 | tf_op jit(solution)/shard_map/products/pallas_call | solution.py:272
  67.8 0.0 copy-start.4
  67.8 3.6 %all-to-all-start.2 = ((f32[8,8,2,8,512]{4,3,2,1,0:T(8,128)}), f32[8,8,2,8,512]{4,3,2,1,0:T(8,128)S(1)}, u32[]{:S(2)}, u32[]{:S(2)}) async-start(f32[8,8,2,8,512]{4,3,2,1,0:T(8,128)} %bitcast.9), calls=%async_computation.2 | async-start | bytes 4194304 | tf_op jit(solution)/shard_map/all_to_all | solution.py:297
  71.4 1.9 %collective-permute-start.2 = (f32[2,2,2,8,512]{4,3,2,1,0:T(8,128)S(1)}, f32[2,2,2,8,512]{4,3,2,1,0:T(8,128)S(1)}, u32[]{:S(2)}, u32[]{:S(2)}) collective-permute-start(f32[2,2,2,8,512]{4,3,2,1,0:T(8,128)S(1)} %pad_maximum_fusion.chip_ref), channel_id=1, source_target_pairs={{0,2},{2,0},{4,6},{6,4},{1,3},{3,1},{5,7},{7,5},{8,10},{10,8},{12,... | collective-permute-start | bytes 393224 | tf_op jit(solution)/shard_map/ppermute | solution.py:295
  73.3 5.8 %collective-permute-done.2.next_ref = f32[2,2,2,8,512]{4,3,2,1,0:T(8,128)S(1)} collective-permute-done((f32[2,2,2,8,512]{4,3,2,1,0:T(8,128)S(1)}, f32[2,2,2,8,512]{4,3,2,1,0:T(8,128)S(1)}, u32[]{:S(2)}, u32[]{:S(2)}) %collective-permute-start.2) | collective-permute-done | bytes 131104 | tf_op jit(solution)/shard_map/ppermute | solution.py:295
  79.2 0.6 choose.1
  79.8 8.3 %collective-permute-start.3 = (f32[2,2,8,512]{3,2,1,0:T(8,128)S(1)}, f32[2,2,8,512]{3,2,1,0:T(8,128)S(1)}, u32[]{:S(2)}, u32[]{:S(2)}) collective-permute-start(f32[2,2,8,512]{3,2,1,0:T(8,128)S(1)} %choose.1), channel_id=1, source_target_pairs={{0,4},{4,0},{2,6},{6,2},{1,5},{5,1},{3,7},{7,3},{8,12},{12,8},{10,... | collective-permute-start | bytes 196616 | tf_op jit(solution)/shard_map/ppermute | solution.py:316
  88.1 7.9 %all-to-all-done.2.in_ref = f32[8,8,2,8,512]{4,3,2,1,0:T(8,128)S(1)} async-done(((f32[8,8,2,8,512]{4,3,2,1,0:T(8,128)}), f32[8,8,2,8,512]{4,3,2,1,0:T(8,128)S(1)}, u32[]{:S(2)}, u32[]{:S(2)}) %all-to-all-start.2) | async-done | bytes 2097184 | tf_op jit(solution)/shard_map/all_to_all | solution.py:297
  96.0 0.8 near_sum.1
  96.8 0.0 collective-permute-done.3.far_ref
  96.8 7.1 %all-to-all-start.3 = ((f32[8,2,8,512]{3,2,1,0:T(8,128)}), f32[8,2,8,512]{3,2,1,0:T(8,128)S(1)}, u32[]{:S(2)}, u32[]{:S(2)}) async-start(f32[8,2,8,512]{3,2,1,0:T(8,128)} %near_sum.1), calls=%async_computation.3 | async-start | bytes 524288 | tf_op jit(solution)/shard_map/all_to_all | solution.py:318
  104.0 1.6 %copy-done.1 = f32[2,512,512]{2,1,0:T(8,128)S(1)} copy-done((f32[2,512,512]{2,1,0:T(8,128)S(1)}, f32[2,512,512]{2,1,0:T(8,128)}, u32[]{:S(2)}) %copy-start.1) | copy-done | bytes 2097176
  105.6 1.5 %shift.1.shifted_ref = f32[2,2,8,512]{3,2,1,0:T(8,128)S(1)} custom-call(s32[2]{0:T(128)S(1)} %pad_add_fusion.place_ref, s32[16]{0:T(128)S(1)} %copy-done.4, f32[2,2,2,8,512]{4,3,2,1,0:T(8,128)S(1)} %pad_maximum_fusion.chip_ref, f32[2,2,2,8,512]{4,3,2,1,0:T(8,128)S(1)} %collective-permute-done.2.next_ref, ...), custom_call_target="tpu_custom_call" | custom-call | flops 50331648 | bytes 3145728 | tf_op jit(solution)/shard_map/shift/pallas_call | solution.py:320
  107.0 6.5 %all-to-all-done.3.back_ref = f32[8,2,8,512]{3,2,1,0:T(8,128)S(1)} async-done(((f32[8,2,8,512]{3,2,1,0:T(8,128)}), f32[8,2,8,512]{3,2,1,0:T(8,128)S(1)}, u32[]{:S(2)}, u32[]{:S(2)}) %all-to-all-start.3) | async-done | bytes 262176 | tf_op jit(solution)/shard_map/all_to_all | solution.py:318
  113.5 1.2 %finish.1 = (f32[2,8,512]{2,1,0:T(8,128)}, f32[2,8,512]{2,1,0:T(8,128)}) custom-call(s32[2]{0:T(128)S(1)} %pad_add_fusion.place_ref, s32[16]{0:T(128)S(1)} %copy-done.5, f32[8,2,8,512]{3,2,1,0:T(8,128)S(1)} %all-to-all-done.3.back_ref, f32[2,2,8,512]{3,2,1,0:T(8,128)S(1)} %shift.1.shifted_ref), custom_call_target="tpu_custom_call" | custom-call | tf_op jit(solution)/shard_map/finish/pallas_call | solution.py:332
  (7 shorter events, 0.0 us)
Async XLA Ops:
  0.6 6.9 %copy-start.2 = (f32[2,8,512]{2,1,0:T(8,128)S(1)}, f32[2,8,512]{2,1,0:T(8,128)}, u32[]{:S(2)}) copy-start(f32[2,8,512]{2,1,0:T(8,128)} %one_ref.1) | copy-start | bytes 98308
  0.6 6.8 %copy-start.3 = (f32[2,8,512]{2,1,0:T(8,128)S(1)}, f32[2,8,512]{2,1,0:T(8,128)}, u32[]{:S(2)}) copy-start(f32[2,8,512]{2,1,0:T(8,128)} %two_ref.1) | copy-start | bytes 98308
  0.7 6.8 %copy-start.5 = (s32[16]{0:T(128)S(1)}, s32[16]{0:T(128)}, u32[]{:S(2)}) copy-start(s32[16]{0:T(128)} %dims_ref.3) | copy-start | bytes 196
  3.1 56.5 %collective-permute-start.1 = (f32[2,512,512]{2,1,0:T(8,128)}, f32[2,512,512]{2,1,0:T(8,128)}, u32[]{:S(2)}, u32[]{:S(2)}) collective-permute-start(f32[2,512,512]{2,1,0:T(8,128)} %pick.1), channel_id=1, source_target_pairs={{0,64},{64,0},{1,65},{65,1},{2,66},{66,2},{3,67},{67,3},{4,68},{68... | collective-permute-start | bytes 6291464 | tf_op jit(solution)/shard_map/ppermute | solution.py:60
  8.8 17.3 %all-to-all-start.1 = ((f32[8,2,8,512]{3,2,1,0:T(8,128)}), f32[8,2,8,512]{3,2,1,0:T(8,128)S(1)}, u32[]{:S(2)}, u32[]{:S(2)}) async-start(f32[8,2,8,512]{3,2,1,0:T(8,128)} %get-tuple-element.17), calls=%async_computation.1 | async-start | bytes 524288 | tf_op jit(solution)/shard_map/all_to_all | solution.py:238
  15.9 3.1 %collective-permute-start = (f32[2,2,8,512]{3,2,1,0:T(8,128)S(1)}, f32[2,2,8,512]{3,2,1,0:T(8,128)S(1)}, u32[]{:S(2)}, u32[]{:S(2)}) collective-permute-start(f32[2,2,8,512]{3,2,1,0:T(8,128)S(1)} %get-tuple-element.18), channel_id=1, source_target_pairs={{0,1},{1,0},{2,3},{3,2},{4,5},{5,4},{6,7},{7,6},{8,9},{9,8},{10,11... | collective-permute-start | bytes 196616 | tf_op jit(solution)/shard_map/ppermute | solution.py:242
  17.8 37.6 %copy-start = (f32[1,2,512,512]{3,2,1,0:T(8,128)S(1)}, f32[1,2,512,512]{3,2,1,0:T(8,128)}, u32[]{:S(2)}) copy-start(f32[1,2,512,512]{3,2,1,0:T(8,128)} %left_ref.1) | copy-start | bytes 6291460
  67.8 11.4 %copy-start.4 = (s32[16]{0:T(128)S(1)}, s32[16]{0:T(128)}, u32[]{:S(2)}) copy-start(s32[16]{0:T(128)} %pair_ref.3) | copy-start | bytes 196
  67.8 28.2 %all-to-all-start.2 = ((f32[8,8,2,8,512]{4,3,2,1,0:T(8,128)}), f32[8,8,2,8,512]{4,3,2,1,0:T(8,128)S(1)}, u32[]{:S(2)}, u32[]{:S(2)}) async-start(f32[8,8,2,8,512]{4,3,2,1,0:T(8,128)} %bitcast.9), calls=%async_computation.2 | async-start | bytes 4194304 | tf_op jit(solution)/shard_map/all_to_all | solution.py:297
  71.4 7.8 %collective-permute-start.2 = (f32[2,2,2,8,512]{4,3,2,1,0:T(8,128)S(1)}, f32[2,2,2,8,512]{4,3,2,1,0:T(8,128)S(1)}, u32[]{:S(2)}, u32[]{:S(2)}) collective-permute-start(f32[2,2,2,8,512]{4,3,2,1,0:T(8,128)S(1)} %pad_maximum_fusion.chip_ref), channel_id=1, source_target_pairs={{0,2},{2,0},{4,6},{6,4},{1,3},{3,1},{5,7},{7,5},{8,10},{10,8},{12,... | collective-permute-start | bytes 393224 | tf_op jit(solution)/shard_map/ppermute | solution.py:295
  79.8 17.0 %collective-permute-start.3 = (f32[2,2,8,512]{3,2,1,0:T(8,128)S(1)}, f32[2,2,8,512]{3,2,1,0:T(8,128)S(1)}, u32[]{:S(2)}, u32[]{:S(2)}) collective-permute-start(f32[2,2,8,512]{3,2,1,0:T(8,128)S(1)} %choose.1), channel_id=1, source_target_pairs={{0,4},{4,0},{2,6},{6,2},{1,5},{5,1},{3,7},{7,3},{8,12},{12,8},{10,... | collective-permute-start | bytes 196616 | tf_op jit(solution)/shard_map/ppermute | solution.py:316
  96.8 16.7 %all-to-all-start.3 = ((f32[8,2,8,512]{3,2,1,0:T(8,128)}), f32[8,2,8,512]{3,2,1,0:T(8,128)S(1)}, u32[]{:S(2)}, u32[]{:S(2)}) async-start(f32[8,2,8,512]{3,2,1,0:T(8,128)} %near_sum.1), calls=%async_computation.3 | async-start | bytes 524288 | tf_op jit(solution)/shard_map/all_to_all | solution.py:318
  104.0 1.6 %copy-start.1 = (f32[2,512,512]{2,1,0:T(8,128)S(1)}, f32[2,512,512]{2,1,0:T(8,128)}, u32[]{:S(2)}) copy-start(f32[2,512,512]{2,1,0:T(8,128)} %shift_ref.1) | copy-start | bytes 6291460

commit v6 on v5

--- a/solution.py
+++ b/solution.py
@@ -19,7 +19,7 @@
 HBM = pl.BlockSpec(memory_space=pl.ANY)
 PARAMS = pltpu.CompilerParams(vmem_limit_bytes=48 * 1024 * 1024)
 OWN = pltpu.CompilerParams(vmem_limit_bytes=46 * 1024 * 1024)
-MAIN = pltpu.CompilerParams(vmem_limit_bytes=48 * 1024 * 1024)
+MAIN = pltpu.CompilerParams(vmem_limit_bytes=47 * 1024 * 1024)
 WIDE = pltpu.CompilerParams(vmem_limit_bytes=60 * 1024 * 1024)
 
 
@@ -94,13 +94,14 @@
                 far_ref[block * 4 + slot, vector] = live
 
 
-def own_kernel(place_ref, g_ref, l_ref, ph, pw, mh, ml, g, left, sems):
+def own_kernel(place_ref, g_ref, l_ref, r_ref, ph, pw, mh, ml, rh, rl, g, left, right, sems):
     width = g.shape[-1]
     half = width // 2
     mine = place_ref[0] // 8 % 2
     loads = [
         pltpu.make_async_copy(g_ref, g, sems.at[0]),
         pltpu.make_async_copy(l_ref.at[0, mine], left, sems.at[1]),
+        pltpu.make_async_copy(r_ref.at[0, mine], right, sems.at[2]),
     ]
     for load in loads:
         load.start()
@@ -119,16 +120,17 @@
         for v in range(2):
             m = times(high, ph[v]) + times(low, ph[v]) + times(high, pw[v])
             mh[v, rows], ml[v, rows] = halves(m)
+    loads[2].wait()
+    rh[...], rl[...] = halves(right[...])
 
 
 def product_kernel(
-    place_ref, ph, pw, own_h, own_l, r_ref, pair_ref, out_ref,
+    place_ref, ph, pw, own_h, own_l, own_rh, own_rl, pair_ref, out_ref,
     ops, out, mh, ml, rh, rl, sems, out_sems,
 ):
     width = ops.shape[-1]
     half = width // 2
-    mine = place_ref[0] // 8 % 2
-    sources = (pair_ref.at[0], r_ref.at[0, mine], pair_ref.at[1])
+    sources = (pair_ref.at[0], pair_ref.at[1])
     loads = [
         pltpu.make_async_copy(source, ops.at[at], sems.at[at]) for at, source in enumerate(sources)
     ]
@@ -141,16 +143,15 @@
         for v in range(2):
             m = times(high, ph[v]) + times(low, ph[v]) + times(high, pw[v])
             mh[v, rows], ml[v, rows] = halves(m)
-    for t in range(2):
-        loads[1 + t].wait()
-        rh[t], rl[t] = halves(ops[1 + t])
+    loads[1].wait()
+    rh[...], rl[...] = halves(ops[1])
     stores = []
     for v in range(2):
         for i in range(2):
             rows = pl.ds(i * half, half)
-            s = times_t(own_h[v, rows], rh[0]) + times_t(own_l[v, rows], rh[0])
-            s += times_t(own_h[v, rows], rl[0]) + times_t(mh[v, rows], rh[1])
-            s += times_t(ml[v, rows], rh[1]) + times_t(mh[v, rows], rl[1])
+            s = times_t(own_h[v, rows], own_rh[...]) + times_t(own_l[v, rows], own_rh[...])
+            s += times_t(own_h[v, rows], own_rl[...]) + times_t(mh[v, rows], rh[...])
+            s += times_t(ml[v, rows], rh[...]) + times_t(mh[v, rows], rl[...])
             s = s.reshape(2, 2, 4, 2, 8, width)
             for xl in range(2):
                 for yl in range(2):
@@ -254,34 +255,35 @@
     half_array = jax.ShapeDtypeStruct((2, width, width), BF16)
     own = pl.pallas_call(
         own_kernel,
-        out_shape=(half_array,) * 4,
-        in_specs=[SMEM, HBM, HBM],
-        out_specs=(VMEM,) * 4,
+        out_shape=(half_array,) * 4 + (jax.ShapeDtypeStruct((width, width), BF16),) * 2,
+        in_specs=[SMEM, HBM, HBM, HBM],
+        out_specs=(VMEM,) * 6,
         scratch_shapes=[
             pltpu.VMEM((4, 2, 2, 4, 2, rows, width), F32),
             pltpu.VMEM((width, width), F32),
-            pltpu.SemaphoreType.DMA((2,)),
+            pltpu.VMEM((width, width), F32),
+            pltpu.SemaphoreType.DMA((3,)),
         ],
         compiler_params=OWN,
         cost_estimate=pl.CostEstimate(
             flops=6 * 2 * 512**3, bytes_accessed=7 * 2**20, transcendentals=0
         ),
         name="own",
-    )(place, near_in.reshape(4, 2, 2, 4, 2, rows, width), left_ops)
+    )(place, near_in.reshape(4, 2, 2, 4, 2, rows, width), left_ops, right_ops)
 
     products = pl.pallas_call(
         product_kernel,
         out_shape=shape(2, 2, 2, 2, 4, 2, rows, width),
-        in_specs=[SMEM, VMEM, VMEM, VMEM, VMEM, HBM, HBM],
+        in_specs=[SMEM] + [VMEM] * 6 + [HBM],
         out_specs=HBM,
         scratch_shapes=[
-            pltpu.VMEM((3, width, width), F32),
+            pltpu.VMEM((2, width, width), F32),
             pltpu.VMEM((2, 2, 2, 2, 4, 2, rows, width), F32),
             pltpu.VMEM((2, width, width), BF16),
             pltpu.VMEM((2, width, width), BF16),
-            pltpu.VMEM((2, width, width), BF16),
-            pltpu.VMEM((2, width, width), BF16),
-            pltpu.SemaphoreType.DMA((3,)),
+            pltpu.VMEM((width, width), BF16),
+            pltpu.VMEM((width, width), BF16),
+            pltpu.SemaphoreType.DMA((2,)),
             pltpu.SemaphoreType.DMA((4,)),
         ],
         compiler_params=MAIN,
@@ -289,7 +291,7 @@
             flops=18 * 2 * 512**3, bytes_accessed=9 * 2**20, transcendentals=0
         ),
         name="products",
-    )(place, *own, right_ops, pair_in)
+    )(place, *own, pair_in)
 
     chip = after(jnp.stack([live, other_core]), near_in)
     next_chip = lax.ppermute(chip, "zh", [(0, 1), (1, 0), (2, 3), (3, 2)])

time: 115 us -> 115 us (level)
  no operation moved by 1% of the time
where the time goes in v6:
time: 115 us
  starting transfers between devices  34.6 us (30%)
  blocking collectives  29 us (25%)
  waiting for transfers between devices  28.3 us (25%)
  Pallas kernels  20.1 us (17%)
  local copies, waits for them, and re-layouts  1.87 us (2%)
    all_to_all x1, blocking collectives, per_device(): lax.all_to_all(jnp.broadcast_to(value[None], (8,) + value.shape), ('xh',...  29 us
    ppermute x1, starting transfers between devices, per_device(): from_far = lax.ppermute(chosen, 'zh', [(0, 2), (2, 0), (1, 3), (3, 1)])  8.46 us
    pallas_call x1, Pallas kernels, per_device(): pl.pallas_call(product_kernel, out_shape=shape(2, 2, 2, 2, 4, 2, rows, wi...  7.99 us
    all_to_all x1, waiting for transfers between devices, per_device(): lax.all_to_all(products.reshape(8, 8, 2, rows, width), ('xh', 'xl', 'yl')...  7.64 us
    all_to_all x1, starting transfers between devices, per_device(): far_back = lax.all_to_all(near_sum, ('zl', 'yh'), 0, 0, tiled=True)  7.26 us
    all_to_all x1, starting transfers between devices, per_device(): lax.all_to_all(far_out, AXES, 0, 0, tiled=True, axis_index_groups=far_gro...  7.1 us
    all_to_all x1, waiting for transfers between devices, per_device(): lax.all_to_all(far_out, AXES, 0, 0, tiled=True, axis_index_groups=far_gro...  7.09 us
    all_to_all x1, waiting for transfers between devices, per_device(): far_back = lax.all_to_all(near_sum, ('zl', 'yh'), 0, 0, tiled=True)  6.51 us
  transfers between devices with their start and end apart: 7, of which 5 were waited for; matrix products, arithmetic and copies ran while one was open for 0% of the time, Pallas kernels for 7%

profile of v6, /device:TPU:128, one launch (start us, length us, event | category | flops | bytes accessed | tf_op | source)
XLA Modules:
  0.0 114.7 jit_solution(16672765600421044917)
XLA Ops:
  0.6 0.0 copy-start.2
  0.7 2.4 %pick.1 = f32[2,512,512]{2,1,0:T(8,128)} custom-call(s32[1]{0:T(128)} %bitcast.3.spot_ref, f32[1,2,512,512]{3,2,1,0:T(8,128)} %left_ref.1, f32[1,2,512,512]{3,2,1,0:T(8,128)} %right_ref.1), custom_call_target="tpu_custom_call" | custom-call | tf_op jit(solution)/shard_map/pick/pallas_call | solution.py:216
  3.1 4.3 %collective-permute-start.1 = (f32[2,512,512]{2,1,0:T(8,128)}, f32[2,512,512]{2,1,0:T(8,128)}, u32[]{:S(2)}, u32[]{:S(2)}) collective-permute-start(f32[2,512,512]{2,1,0:T(8,128)} %pick.1), channel_id=1, source_target_pairs={{0,64},{64,0},{1,65},{65,1},{2,66},{66,2},{3,67},{67,3},{4,68},{68... | collective-permute-start | bytes 6291464 | tf_op jit(solution)/shard_map/ppermute | solution.py:60
  7.4 0.1 pad_add_fusion.place_ref
  7.5 0.0 copy-done.2
  7.5 0.0 copy-done.5
  7.5 1.3 %spread.1 = (f32[8,2,8,512]{3,2,1,0:T(8,128)}, f32[2,2,8,512]{3,2,1,0:T(8,128)S(1)}) custom-call(s32[2]{0:T(128)S(1)} %pad_add_fusion.place_ref, s32[16]{0:T(128)S(1)} %copy-done.5, f32[2,8,512]{2,1,0:T(8,128)S(1)} %copy-done.2, f32[2,8,512]{2,1,0:T(8,128)S(1)} %copy-done.3), custom_call_target="tpu_custom_call" | custom-call | tf_op jit(solution)/shard_map/spread/pallas_call | solution.py:231
  8.8 7.1 %all-to-all-start.1 = ((f32[8,2,8,512]{3,2,1,0:T(8,128)}), f32[8,2,8,512]{3,2,1,0:T(8,128)S(1)}, u32[]{:S(2)}, u32[]{:S(2)}) async-start(f32[8,2,8,512]{3,2,1,0:T(8,128)} %get-tuple-element.19), calls=%async_computation.1 | async-start | bytes 524288 | tf_op jit(solution)/shard_map/all_to_all | solution.py:239
  15.9 1.9 %collective-permute-start = (f32[2,2,8,512]{3,2,1,0:T(8,128)S(1)}, f32[2,2,8,512]{3,2,1,0:T(8,128)S(1)}, u32[]{:S(2)}, u32[]{:S(2)}) collective-permute-start(f32[2,2,8,512]{3,2,1,0:T(8,128)S(1)} %get-tuple-element.20), channel_id=1, source_target_pairs={{0,1},{1,0},{2,3},{3,2},{4,5},{5,4},{6,7},{7,6},{8,9},{9,8},{10,11... | collective-permute-start | bytes 196616 | tf_op jit(solution)/shard_map/ppermute | solution.py:243
  17.8 0.0 copy-start
  17.8 1.2 %collective-permute-done = f32[2,2,8,512]{3,2,1,0:T(8,128)S(1)} collective-permute-done((f32[2,2,8,512]{3,2,1,0:T(8,128)S(1)}, f32[2,2,8,512]{3,2,1,0:T(8,128)S(1)}, u32[]{:S(2)}, u32[]{:S(2)}) %collective-permute-start) | collective-permute-done | bytes 65568 | tf_op jit(solution)/shard_map/ppermute | solution.py:243
  19.0 7.1 %all-to-all-done.1 = f32[8,2,8,512]{3,2,1,0:T(8,128)S(1)} async-done(((f32[8,2,8,512]{3,2,1,0:T(8,128)}), f32[8,2,8,512]{3,2,1,0:T(8,128)S(1)}, u32[]{:S(2)}, u32[]{:S(2)}) %all-to-all-start.1) | async-done | bytes 262176 | tf_op jit(solution)/shard_map/all_to_all | solution.py:239
  26.1 29.2 %conditional.1 = (f32[8,8,2,8,512]{4,3,2,1,0:T(8,128)}) conditional(s32[]{:T(128)} %convert_element_type.3, () %tuple.16, f32[8,2,8,512]{3,2,1,0:T(8,128)S(1)} %all-to-all-done.1), branch_computations={%region_0.0_spmd, %region_1.0_spmd} | conditional | bytes 6553608 | solution.py:246
  26.1 0.3 broadcast_in_dim.0
  26.4 29.0 %all_to_all.19 = f32[8,8,2,8,512]{4,3,2,1,0:T(8,128)} all-to-all(f32[8,8,2,8,512]{4,3,2,1,0:T(8,128)S(1)} %broadcast_in_dim.0), channel_id=1, replica_groups=mesh['xh'=2,'xl'=2,'zl'=2,'yh'=4,'yl'=2,'zh'=4,'c'=2] {'xh','xl','yl'}, dimensions={0} | all-to-all | bytes 4194304 | tf_op jit(solution)/shard_map/cond/branch_1_fun/all_to_all | solution.py:248
  55.4 4.4 %own.1 = (bf16[2,512,512]{2,1,0:T(8,128)(2,1)S(1)}, bf16[2,512,512]{2,1,0:T(8,128)(2,1)S(1)}, bf16[2,512,512]{2,1,0:T(8,128)(2,1)S(1)}, bf16[2,512,512]{2,1,0:T(...) custom-call(s32[2]{0:T(128)S(1)} %pad_add_fusion.place_ref, ...), custom_call_target="tpu_custom_call" | custom-call | flops 1610612736 | bytes 7340032 | tf_op jit(solution)/shard_map/own/pallas_call | solution.py:256
  59.7 0.0 collective-permute-done.1.pair_ref
  59.8 8.0 %products.1 = f32[2,2,2,2,4,2,8,512]{7,6,5,4,3,2,1,0:T(8,128)} custom-call(s32[2]{0:T(128)S(1)} %pad_add_fusion.place_ref, bf16[2,512,512]{2,1,0:T(8,128)(2,1)S(1)} %get-tuple-element.22.ph, bf16[2,512,512]{2,1,0:T(8,128)(2,1)S(1)} %get-tuple-element.23.pw, bf16[2,512,512]{2,1,0:T(8,128)(2,1)S(1)} %get-tuple-element.24.own_h, ...), custom_call_target="tpu_custom_call" | custom-call | flops 4831838208 | bytes 9437184 | tf_op jit(solution)/shard_map/products/pallas_call | solution.py:274
  67.8 0.0 copy-start.4
  67.8 3.6 %all-to-all-start.2 = ((f32[8,8,2,8,512]{4,3,2,1,0:T(8,128)}), f32[8,8,2,8,512]{4,3,2,1,0:T(8,128)S(1)}, u32[]{:S(2)}, u32[]{:S(2)}) async-start(f32[8,8,2,8,512]{4,3,2,1,0:T(8,128)} %bitcast.9), calls=%async_computation.2 | async-start | bytes 4194304 | tf_op jit(solution)/shard_map/all_to_all | solution.py:299
  71.4 1.9 %collective-permute-start.2 = (f32[2,2,2,8,512]{4,3,2,1,0:T(8,128)S(1)}, f32[2,2,2,8,512]{4,3,2,1,0:T(8,128)S(1)}, u32[]{:S(2)}, u32[]{:S(2)}) collective-permute-start(f32[2,2,2,8,512]{4,3,2,1,0:T(8,128)S(1)} %pad_maximum_fusion.chip_ref), channel_id=1, source_target_pairs={{0,2},{2,0},{4,6},{6,4},{1,3},{3,1},{5,7},{7,5},{8,10},{10,8},{12,... | collective-permute-start | bytes 393224 | tf_op jit(solution)/shard_map/ppermute | solution.py:297
  73.3 5.8 %collective-permute-done.2.next_ref = f32[2,2,2,8,512]{4,3,2,1,0:T(8,128)S(1)} collective-permute-done((f32[2,2,2,8,512]{4,3,2,1,0:T(8,128)S(1)}, f32[2,2,2,8,512]{4,3,2,1,0:T(8,128)S(1)}, u32[]{:S(2)}, u32[]{:S(2)}) %collective-permute-start.2) | collective-permute-done | bytes 131104 | tf_op jit(solution)/shard_map/ppermute | solution.py:297
  79.2 0.6 choose.1
  79.8 8.5 %collective-permute-start.3 = (f32[2,2,8,512]{3,2,1,0:T(8,128)S(1)}, f32[2,2,8,512]{3,2,1,0:T(8,128)S(1)}, u32[]{:S(2)}, u32[]{:S(2)}) collective-permute-start(f32[2,2,8,512]{3,2,1,0:T(8,128)S(1)} %choose.1), channel_id=1, source_target_pairs={{0,4},{4,0},{2,6},{6,2},{1,5},{5,1},{3,7},{7,3},{8,12},{12,8},{10,... | collective-permute-start | bytes 196616 | tf_op jit(solution)/shard_map/ppermute | solution.py:318
  88.2 7.6 %all-to-all-done.2.in_ref = f32[8,8,2,8,512]{4,3,2,1,0:T(8,128)S(1)} async-done(((f32[8,8,2,8,512]{4,3,2,1,0:T(8,128)}), f32[8,8,2,8,512]{4,3,2,1,0:T(8,128)S(1)}, u32[]{:S(2)}, u32[]{:S(2)}) %all-to-all-start.2) | async-done | bytes 2097184 | tf_op jit(solution)/shard_map/all_to_all | solution.py:299
  95.9 0.8 near_sum.1
  96.7 0.0 collective-permute-done.3.far_ref
  96.7 7.3 %all-to-all-start.3 = ((f32[8,2,8,512]{3,2,1,0:T(8,128)}), f32[8,2,8,512]{3,2,1,0:T(8,128)S(1)}, u32[]{:S(2)}, u32[]{:S(2)}) async-start(f32[8,2,8,512]{3,2,1,0:T(8,128)} %near_sum.1), calls=%async_computation.3 | async-start | bytes 524288 | tf_op jit(solution)/shard_map/all_to_all | solution.py:320
  104.0 1.6 %copy-done.1 = f32[2,512,512]{2,1,0:T(8,128)S(1)} copy-done((f32[2,512,512]{2,1,0:T(8,128)S(1)}, f32[2,512,512]{2,1,0:T(8,128)}, u32[]{:S(2)}) %copy-start.1) | copy-done | bytes 2097176
  105.5 1.5 %shift.1.shifted_ref = f32[2,2,8,512]{3,2,1,0:T(8,128)S(1)} custom-call(s32[2]{0:T(128)S(1)} %pad_add_fusion.place_ref, s32[16]{0:T(128)S(1)} %copy-done.4, f32[2,2,2,8,512]{4,3,2,1,0:T(8,128)S(1)} %pad_maximum_fusion.chip_ref, f32[2,2,2,8,512]{4,3,2,1,0:T(8,128)S(1)} %collective-permute-done.2.next_ref, ...), custom_call_target="tpu_custom_call" | custom-call | flops 50331648 | bytes 3145728 | tf_op jit(solution)/shard_map/shift/pallas_call | solution.py:322
  107.0 6.5 %all-to-all-done.3.back_ref = f32[8,2,8,512]{3,2,1,0:T(8,128)S(1)} async-done(((f32[8,2,8,512]{3,2,1,0:T(8,128)}), f32[8,2,8,512]{3,2,1,0:T(8,128)S(1)}, u32[]{:S(2)}, u32[]{:S(2)}) %all-to-all-start.3) | async-done | bytes 262176 | tf_op jit(solution)/shard_map/all_to_all | solution.py:320
  113.5 1.2 %finish.1 = (f32[2,8,512]{2,1,0:T(8,128)}, f32[2,8,512]{2,1,0:T(8,128)}) custom-call(s32[2]{0:T(128)S(1)} %pad_add_fusion.place_ref, s32[16]{0:T(128)S(1)} %copy-done.5, f32[8,2,8,512]{3,2,1,0:T(8,128)S(1)} %all-to-all-done.3.back_ref, f32[2,2,8,512]{3,2,1,0:T(8,128)S(1)} %shift.1.shifted_ref), custom_call_target="tpu_custom_call" | custom-call | tf_op jit(solution)/shard_map/finish/pallas_call | solution.py:334
  (7 shorter events, 0.0 us)
Async XLA Ops:
  0.6 6.9 %copy-start.2 = (f32[2,8,512]{2,1,0:T(8,128)S(1)}, f32[2,8,512]{2,1,0:T(8,128)}, u32[]{:S(2)}) copy-start(f32[2,8,512]{2,1,0:T(8,128)} %one_ref.1) | copy-start | bytes 98308
  0.6 6.8 %copy-start.3 = (f32[2,8,512]{2,1,0:T(8,128)S(1)}, f32[2,8,512]{2,1,0:T(8,128)}, u32[]{:S(2)}) copy-start(f32[2,8,512]{2,1,0:T(8,128)} %two_ref.1) | copy-start | bytes 98308
  0.7 6.8 %copy-start.5 = (s32[16]{0:T(128)S(1)}, s32[16]{0:T(128)}, u32[]{:S(2)}) copy-start(s32[16]{0:T(128)} %dims_ref.3) | copy-start | bytes 196
  3.1 56.6 %collective-permute-start.1 = (f32[2,512,512]{2,1,0:T(8,128)}, f32[2,512,512]{2,1,0:T(8,128)}, u32[]{:S(2)}, u32[]{:S(2)}) collective-permute-start(f32[2,512,512]{2,1,0:T(8,128)} %pick.1), channel_id=1, source_target_pairs={{0,64},{64,0},{1,65},{65,1},{2,66},{66,2},{3,67},{67,3},{4,68},{68... | collective-permute-start | bytes 6291464 | tf_op jit(solution)/shard_map/ppermute | solution.py:60
  8.8 17.3 %all-to-all-start.1 = ((f32[8,2,8,512]{3,2,1,0:T(8,128)}), f32[8,2,8,512]{3,2,1,0:T(8,128)S(1)}, u32[]{:S(2)}, u32[]{:S(2)}) async-start(f32[8,2,8,512]{3,2,1,0:T(8,128)} %get-tuple-element.19), calls=%async_computation.1 | async-start | bytes 524288 | tf_op jit(solution)/shard_map/all_to_all | solution.py:239
  15.9 3.1 %collective-permute-start = (f32[2,2,8,512]{3,2,1,0:T(8,128)S(1)}, f32[2,2,8,512]{3,2,1,0:T(8,128)S(1)}, u32[]{:S(2)}, u32[]{:S(2)}) collective-permute-start(f32[2,2,8,512]{3,2,1,0:T(8,128)S(1)} %get-tuple-element.20), channel_id=1, source_target_pairs={{0,1},{1,0},{2,3},{3,2},{4,5},{5,4},{6,7},{7,6},{8,9},{9,8},{10,11... | collective-permute-start | bytes 196616 | tf_op jit(solution)/shard_map/ppermute | solution.py:243
  17.8 37.6 %copy-start = (f32[1,2,512,512]{3,2,1,0:T(8,128)S(1)}, f32[1,2,512,512]{3,2,1,0:T(8,128)}, u32[]{:S(2)}) copy-start(f32[1,2,512,512]{3,2,1,0:T(8,128)} %left_ref.1) | copy-start | bytes 6291460
  67.8 11.4 %copy-start.4 = (s32[16]{0:T(128)S(1)}, s32[16]{0:T(128)}, u32[]{:S(2)}) copy-start(s32[16]{0:T(128)} %pair_ref.3) | copy-start | bytes 196
  67.8 28.1 %all-to-all-start.2 = ((f32[8,8,2,8,512]{4,3,2,1,0:T(8,128)}), f32[8,8,2,8,512]{4,3,2,1,0:T(8,128)S(1)}, u32[]{:S(2)}, u32[]{:S(2)}) async-start(f32[8,8,2,8,512]{4,3,2,1,0:T(8,128)} %bitcast.9), calls=%async_computation.2 | async-start | bytes 4194304 | tf_op jit(solution)/shard_map/all_to_all | solution.py:299
  71.4 7.8 %collective-permute-start.2 = (f32[2,2,2,8,512]{4,3,2,1,0:T(8,128)S(1)}, f32[2,2,2,8,512]{4,3,2,1,0:T(8,128)S(1)}, u32[]{:S(2)}, u32[]{:S(2)}) collective-permute-start(f32[2,2,2,8,512]{4,3,2,1,0:T(8,128)S(1)} %pad_maximum_fusion.chip_ref), channel_id=1, source_target_pairs={{0,2},{2,0},{4,6},{6,4},{1,3},{3,1},{5,7},{7,5},{8,10},{10,8},{12,... | collective-permute-start | bytes 393224 | tf_op jit(solution)/shard_map/ppermute | solution.py:297
  79.8 16.9 %collective-permute-start.3 = (f32[2,2,8,512]{3,2,1,0:T(8,128)S(1)}, f32[2,2,8,512]{3,2,1,0:T(8,128)S(1)}, u32[]{:S(2)}, u32[]{:S(2)}) collective-permute-start(f32[2,2,8,512]{3,2,1,0:T(8,128)S(1)} %choose.1), channel_id=1, source_target_pairs={{0,4},{4,0},{2,6},{6,2},{1,5},{5,1},{3,7},{7,3},{8,12},{12,8},{10,... | collective-permute-start | bytes 196616 | tf_op jit(solution)/shard_map/ppermute | solution.py:318
  96.7 16.9 %all-to-all-start.3 = ((f32[8,2,8,512]{3,2,1,0:T(8,128)}), f32[8,2,8,512]{3,2,1,0:T(8,128)S(1)}, u32[]{:S(2)}, u32[]{:S(2)}) async-start(f32[8,2,8,512]{3,2,1,0:T(8,128)} %near_sum.1), calls=%async_computation.3 | async-start | bytes 524288 | tf_op jit(solution)/shard_map/all_to_all | solution.py:320
  104.0 1.6 %copy-start.1 = (f32[2,512,512]{2,1,0:T(8,128)S(1)}, f32[2,512,512]{2,1,0:T(8,128)}, u32[]{:S(2)}) copy-start(f32[2,512,512]{2,1,0:T(8,128)} %shift_ref.1) | copy-start | bytes 6291460
